TPU v7x, 32 devices: a whole 2x2x4 slice. The times are simulated.
32 devices in a mesh: dp: 16 (over z, x, core), seq: 2 (over y).
Axes of the slice: x: 2, y: 2, z: 4, core: 2. Of those that a mesh axis runs over, the one named last changes fastest.
Arguments:
- hidden_in: bfloat16 [16, 1024, 1024], P('dp', 'seq'), may hold values from -6 to 6
- condition: bfloat16 [16, 1024], P('dp'), may hold values from -6 to 6
- cotangent: bfloat16 [16, 1024, 1024], P('dp', 'seq'), as said below
- weights_in: float32 [1024, 14336], P('seq', 'dp')
- weights_down: float32 [4096, 1024], P('seq', 'dp'), may hold values from -0.09375 to 0.09375
- biases: float32 [14336], P(('dp', 'seq')), may hold values from -1.8 to 1.8
- moment_in: float32 [1024, 14336], P('seq', 'dp'), as said below
- moment_down: float32 [4096, 1024], P('seq', 'dp'), as said below
- moment_bias: float32 [14336], P(('dp', 'seq')), as said below
- square_in: float32 [1024, 14336], P('seq', 'dp'), as said below
- square_down: float32 [4096, 1024], P('seq', 'dp'), as said below
- square_bias: float32 [14336], P(('dp', 'seq')), as said below
Outputs:
- block_out: bfloat16 [16, 1024, 1024], P('dp', 'seq')
- input_grad: float32 [16, 1024, 1024], P('dp', 'seq')
- cond_grad: float32 [16, 1024], P('dp')
- moments_in: float32 [1024, 14336], P('seq', 'dp')
- moments_down: float32 [4096, 1024], P('seq', 'dp')
- moments_bias: float32 [14336], P(('dp', 'seq'))
- squares_in: float32 [1024, 14336], P('seq', 'dp')
- squares_down: float32 [4096, 1024], P('seq', 'dp')
- squares_bias: float32 [14336], P(('dp', 'seq'))
- master_in: float32 [1024, 14336], P('seq', 'dp')
- master_down: float32 [4096, 1024], P('seq', 'dp')
- master_bias: float32 [14336], P(('dp', 'seq'))
- copy_in: bfloat16 [1024, 14336], P('seq', 'dp')
- copy_down: bfloat16 [4096, 1024], P('seq', 'dp')
- copy_bias: bfloat16 [14336], P(('dp', 'seq'))
Inputs may be any that keep to these rules, and one draw needn't show every extreme that they name: A cotangent of order one in every token. `moment_in`: real first moments of both signs. `moment_down`: real first moments of both signs. `moment_bias`: real first moments of both signs. `square_in`: positive second moments. `square_down`: positive second moments. `square_bias`: positive second moments.
All inputs are finite; a program needn't handle non-finite values.
Results may differ from a plain program's by a relative error of at most 0.025.
Values may be sent and summed in bfloat16 or wider, within the bound.
A program may use at most 384 MiB of HBM per device.

v0:
```python
import math

import jax
import jax.numpy as jnp
from jax import lax
from jax.sharding import PartitionSpec as P

D = 1024
HEADS = 16
HEAD_DIM = 64
FF = 4096
STEP = 5


norm_eps = 1e-06
beta_first = 0.5
beta_second = 0.5
adam_eps = 1e-08
weight_decay = 0.01
rate_in = 0.03
rate_down = 0.016
rate_bias = 0.3


def layer_norm(values):
    center = values - jnp.mean(values, axis=-1, keepdims=True)
    return center * lax.rsqrt(jnp.mean(center * center, axis=-1, keepdims=True) + norm_eps)


def adamw_step(master, moment, square, gradient, step_rate):
    moment_new = beta_first * moment + (1.0 - beta_first) * gradient
    square_new = beta_second * square + (1.0 - beta_second) * gradient * gradient
    corrected = moment_new / (1.0 - beta_first**STEP)
    scale_sq = square_new / (1.0 - beta_second**STEP)
    master_new = master - step_rate * (
        corrected / (jnp.sqrt(scale_sq) + adam_eps) + weight_decay * master
    )
    return (moment_new, square_new, master_new)


def dense_map(values, matrix):
    return jnp.einsum("nld,de->nle", values, matrix, preferred_element_type=jnp.float32)


def dense_back(gradients, matrix):
    return jnp.einsum("nle,de->nld", gradients, matrix, preferred_element_type=jnp.float32)


def outer_sum(values, gradients):
    return jnp.einsum("nld,nle->de", values, gradients, preferred_element_type=jnp.float32)


def total_sum(values):
    return jnp.sum(values.astype(jnp.float32), axis=(0, 1))


def gather_weights(low_in, low_down, low_bias):
    seq_parts = (
        lax.all_gather(low_in, "seq", axis=0, tiled=True),
        lax.all_gather(low_down, "seq", axis=0, tiled=True),
        lax.all_gather(low_bias, "seq", axis=0, tiled=True),
    )
    whole_in, whole_down, bias_row = (
        lax.all_gather(seq_parts[0], "dp", axis=1, tiled=True),
        lax.all_gather(seq_parts[1], "dp", axis=1, tiled=True),
        lax.all_gather(seq_parts[2].reshape(1, -1), "dp", axis=1, tiled=True),
    )
    return (whole_in, whole_down, bias_row[0])


def head_layout():
    heads_here = math.gcd(HEADS, max(1, 128 // HEAD_DIM))
    return (heads_here, heads_here * HEAD_DIM, HEADS // heads_here)


def split_heads(values, lane_start, lane_count, heads_here):
    piece = lax.dynamic_slice_in_dim(values, lane_start, lane_count, 2)
    return piece.reshape(piece.shape[0], piece.shape[1], heads_here, HEAD_DIM)


def join_heads(stacked):
    moved = jnp.moveaxis(stacked, 0, 2)
    return moved.reshape(moved.shape[0], moved.shape[1], moved.shape[2] * moved.shape[3])


def attention_forward(queries, keys_all, values_all):
    heads_here, lane_count, head_steps = head_layout()
    scale_factor = HEAD_DIM ** (-0.5)

    def one_group(group_index):
        lane_start = group_index * lane_count
        query_part = split_heads(queries, lane_start, lane_count, heads_here)
        key_part = split_heads(keys_all, lane_start, lane_count, heads_here)
        value_part = split_heads(values_all, lane_start, lane_count, heads_here)
        scores = (
            jnp.einsum("nqhd,nkhd->nhqk", query_part, key_part, preferred_element_type=jnp.float32)
            * scale_factor
        )
        row_max = jnp.max(scores, axis=-1, keepdims=True)
        exponent = jnp.exp(scores - row_max)
        row_total = jnp.sum(exponent, axis=-1, keepdims=True)
        weights = (exponent / row_total).astype(jnp.bfloat16)
        attn_part = jnp.einsum(
            "nhqk,nkhd->nqhd", weights, value_part, preferred_element_type=jnp.float32
        )
        shaped = attn_part.reshape(attn_part.shape[0], attn_part.shape[1], lane_count)
        return (shaped, (row_max + jnp.log(row_total))[..., 0])

    stacked, log_totals = lax.map(one_group, jnp.arange(head_steps))
    return (join_heads(stacked), log_totals)


def attention_backward(queries, keys_all, values_all, log_totals, grad_mixed):
    heads_here, lane_count, head_steps = head_layout()
    scale_factor = HEAD_DIM ** (-0.5)

    def one_group(carried):
        group_index, log_part = carried
        lane_start = group_index * lane_count
        query_part = split_heads(queries, lane_start, lane_count, heads_here)
        key_part = split_heads(keys_all, lane_start, lane_count, heads_here)
        value_part = split_heads(values_all, lane_start, lane_count, heads_here)
        grad_part = split_heads(grad_mixed, lane_start, lane_count, heads_here)
        scores = (
            jnp.einsum("nqhd,nkhd->nhqk", query_part, key_part, preferred_element_type=jnp.float32)
            * scale_factor
        )
        probability = jnp.exp(scores - log_part[..., None])
        grad_prob = jnp.einsum(
            "nqhd,nkhd->nhqk", grad_part, value_part, preferred_element_type=jnp.float32
        )
        inner_sum = jnp.sum(probability * grad_prob, axis=-1, keepdims=True)
        grad_score = (probability * (grad_prob - inner_sum)).astype(jnp.bfloat16)
        grad_query = (
            jnp.einsum("nhqk,nkhd->nqhd", grad_score, key_part, preferred_element_type=jnp.float32)
            * scale_factor
        )
        grad_key = (
            jnp.einsum(
                "nhqk,nqhd->nkhd", grad_score, query_part, preferred_element_type=jnp.float32
            )
            * scale_factor
        )
        grad_value = jnp.einsum(
            "nhqk,nqhd->nkhd",
            probability.astype(jnp.bfloat16),
            grad_part,
            preferred_element_type=jnp.float32,
        )
        return (
            grad_query.reshape(grad_query.shape[0], grad_query.shape[1], lane_count),
            grad_key.reshape(grad_key.shape[0], grad_key.shape[1], lane_count),
            grad_value.reshape(grad_value.shape[0], grad_value.shape[1], lane_count),
        )

    query_terms, key_terms, value_terms = lax.map(one_group, (jnp.arange(head_steps), log_totals))
    return (join_heads(query_terms), join_heads(key_terms), join_heads(value_terms))


def local(
    hidden_in,
    condition,
    cotangent,
    weights_in,
    weights_down,
    biases,
    moment_in,
    moment_down,
    moment_bias,
    square_in,
    square_down,
    square_bias,
):
    low_in = weights_in.astype(jnp.bfloat16)
    low_down = weights_down.astype(jnp.bfloat16)
    low_bias = biases.astype(jnp.bfloat16)
    whole_in, whole_down, bias_all = gather_weights(low_in, low_down, low_bias)
    bias_float = bias_all.astype(jnp.float32)
    hidden = hidden_in.astype(jnp.float32)
    cond_float = condition.astype(jnp.float32)
    cond_act = jax.nn.silu(cond_float).astype(jnp.bfloat16)
    modulation = (
        jnp.dot(cond_act, whole_in[:, : 6 * D], preferred_element_type=jnp.float32)
        + bias_float[: 6 * D]
    )
    pieces = [modulation[:, None, part_index * D : (part_index + 1) * D] for part_index in range(6)]
    shift_one, scale_one, gate_one, shift_two, scale_two, gate_two = pieces
    normed_one = layer_norm(hidden)
    input_one = (normed_one * (1.0 + scale_one) + shift_one).astype(jnp.bfloat16)
    qkv_all = dense_map(input_one, whole_in[:, 6 * D : 9 * D])
    queries = (qkv_all[..., :D] + bias_float[6 * D : 7 * D]).astype(jnp.bfloat16)
    keys_local = qkv_all[..., D : 2 * D].astype(jnp.bfloat16)
    values_local = (qkv_all[..., 2 * D :] + bias_float[7 * D : 8 * D]).astype(jnp.bfloat16)
    keys_all, values_all = (
        lax.all_gather(keys_local, "seq", axis=1, tiled=True),
        lax.all_gather(values_local, "seq", axis=1, tiled=True),
    )
    attn_float, log_totals = attention_forward(queries, keys_all, values_all)
    attn_mixed = attn_float.astype(jnp.bfloat16)
    attn_out = dense_map(attn_mixed, whole_in[:, 9 * D : 10 * D]) + bias_float[8 * D : 9 * D]
    middle = hidden + gate_one * attn_out
    normed_two = layer_norm(middle)
    input_two = (normed_two * (1.0 + scale_two) + shift_two).astype(jnp.bfloat16)
    upward = dense_map(input_two, whole_in[:, 10 * D :]) + bias_float[9 * D : 9 * D + FF]
    activated = jax.nn.gelu(upward, approximate=True).astype(jnp.bfloat16)
    branch = dense_map(activated, whole_down) + bias_float[9 * D + FF :]
    block_out = (middle + gate_two * branch).astype(jnp.bfloat16)
    whole_in, whole_down, bias_all = gather_weights(low_in, low_down, low_bias)
    grad_out = cotangent.astype(jnp.float32)
    grad_branch = (grad_out * gate_two).astype(jnp.bfloat16)
    gate_two_grad = jnp.sum(grad_out * branch, axis=1)
    grad_down = outer_sum(activated, grad_branch)
    bias_down_grad = total_sum(grad_branch)
    grad_act = dense_back(grad_branch, whole_down)
    _, gelu_pull = jax.vjp(lambda inner_value: jax.nn.gelu(inner_value, approximate=True), upward)
    grad_upward = gelu_pull(grad_act)[0].astype(jnp.bfloat16)
    grad_up = outer_sum(input_two, grad_upward)
    bias_up_grad = total_sum(grad_upward)
    grad_input_two = dense_back(grad_upward, whole_in[:, 10 * D :])
    shift_two_grad = jnp.sum(grad_input_two, axis=1)
    scale_two_grad = jnp.sum(grad_input_two * normed_two, axis=1)
    _, norm_pull_two = jax.vjp(layer_norm, middle)
    grad_middle = grad_out + norm_pull_two(grad_input_two * (1.0 + scale_two))[0]
    grad_attn = (grad_middle * gate_one).astype(jnp.bfloat16)
    gate_one_grad = jnp.sum(grad_middle * attn_out, axis=1)
    grad_out_proj = outer_sum(attn_mixed, grad_attn)
    bias_out_grad = total_sum(grad_attn)
    grad_mixed = dense_back(grad_attn, whole_in[:, 9 * D : 10 * D]).astype(jnp.bfloat16)
    grad_query, key_terms, value_terms = attention_backward(
        queries, keys_all, values_all, log_totals, grad_mixed
    )
    key_grad, value_grad = (
        lax.psum_scatter(
            key_terms.astype(jnp.bfloat16), "seq", scatter_dimension=1, tiled=True
        ).astype(jnp.float32),
        lax.psum_scatter(
            value_terms.astype(jnp.bfloat16), "seq", scatter_dimension=1, tiled=True
        ).astype(jnp.float32),
    )
    grad_qkv = jnp.concatenate(
        [
            grad_query.astype(jnp.bfloat16),
            key_grad.astype(jnp.bfloat16),
            value_grad.astype(jnp.bfloat16),
        ],
        axis=-1,
    )
    grad_proj_qkv = outer_sum(input_one, grad_qkv)
    bias_query_grad = total_sum(grad_qkv[..., :D])
    bias_value_grad = total_sum(grad_qkv[..., 2 * D :])
    grad_input_one = dense_back(grad_qkv, whole_in[:, 6 * D : 9 * D])
    shift_one_grad = jnp.sum(grad_input_one, axis=1)
    scale_one_grad = jnp.sum(grad_input_one * normed_one, axis=1)
    _, norm_pull_one = jax.vjp(layer_norm, hidden)
    input_grad = grad_middle + norm_pull_one(grad_input_one * (1.0 + scale_one))[0]
    mod_terms = jnp.concatenate(
        [
            shift_one_grad,
            scale_one_grad,
            gate_one_grad,
            shift_two_grad,
            scale_two_grad,
            gate_two_grad,
        ],
        axis=-1,
    )
    mod_grad = lax.psum(mod_terms, "seq").astype(jnp.bfloat16)
    _, silu_pull = jax.vjp(jax.nn.silu, cond_float)
    cond_grad = silu_pull(
        jnp.einsum("ne,de->nd", mod_grad, whole_in[:, : 6 * D], preferred_element_type=jnp.float32)
    )[0]
    owner_mask = (lax.axis_index("seq") == 0).astype(jnp.float32)
    grad_ada = (
        jnp.einsum("nd,ne->de", cond_act, mod_grad, preferred_element_type=jnp.float32) * owner_mask
    )
    bias_ada_grad = jnp.sum(mod_grad.astype(jnp.float32), axis=0) * owner_mask
    grad_in_all = jnp.zeros((D, 10 * D + FF), jnp.float32)
    grad_in_all = grad_in_all.at[:, : 6 * D].set(grad_ada)
    grad_in_all = grad_in_all.at[:, 6 * D : 9 * D].set(grad_proj_qkv)
    grad_in_all = grad_in_all.at[:, 9 * D : 10 * D].set(grad_out_proj)
    grad_in_all = grad_in_all.at[:, 10 * D :].set(grad_up)
    bias_flat = jnp.concatenate(
        [
            bias_ada_grad,
            bias_query_grad,
            bias_value_grad,
            bias_out_grad,
            bias_up_grad,
            bias_down_grad,
        ]
    )
    summed_in, summed_down, summed_bias = (
        lax.psum_scatter(
            grad_in_all.astype(jnp.bfloat16), "dp", scatter_dimension=1, tiled=True
        ).astype(jnp.float32),
        lax.psum_scatter(
            grad_down.astype(jnp.bfloat16), "dp", scatter_dimension=1, tiled=True
        ).astype(jnp.float32),
        lax.psum_scatter(
            bias_flat.reshape(1, -1).astype(jnp.bfloat16), "dp", scatter_dimension=1, tiled=True
        ).astype(jnp.float32),
    )
    owned_in, owned_down, owned_bias = (
        lax.psum_scatter(
            summed_in.astype(jnp.bfloat16), "seq", scatter_dimension=0, tiled=True
        ).astype(jnp.float32),
        lax.psum_scatter(
            summed_down.astype(jnp.bfloat16), "seq", scatter_dimension=0, tiled=True
        ).astype(jnp.float32),
        lax.psum_scatter(
            summed_bias.reshape(-1).astype(jnp.bfloat16), "seq", scatter_dimension=0, tiled=True
        ).astype(jnp.float32),
    )
    moments_in, squares_in, master_in = adamw_step(
        weights_in, moment_in, square_in, owned_in, rate_in
    )
    moments_down, squares_down, master_down = adamw_step(
        weights_down, moment_down, square_down, owned_down, rate_down
    )
    moments_bias, squares_bias, master_bias = adamw_step(
        biases, moment_bias, square_bias, owned_bias, rate_bias
    )
    return (
        block_out,
        input_grad,
        cond_grad,
        moments_in,
        moments_down,
        moments_bias,
        squares_in,
        squares_down,
        squares_bias,
        master_in,
        master_down,
        master_bias,
        master_in.astype(jnp.bfloat16),
        master_down.astype(jnp.bfloat16),
        master_bias.astype(jnp.bfloat16),
    )


def solution(mesh):
    return jax.shard_map(
        local,
        mesh=mesh,
        in_specs=(
            P("dp", "seq", None),
            P("dp", None),
            P("dp", "seq", None),
            P("seq", "dp"),
            P("seq", "dp"),
            P(("dp", "seq")),
            P("seq", "dp"),
            P("seq", "dp"),
            P(("dp", "seq")),
            P("seq", "dp"),
            P("seq", "dp"),
            P(("dp", "seq")),
        ),
        out_specs=(
            P("dp", "seq", None),
            P("dp", "seq", None),
            P("dp", None),
            P("seq", "dp"),
            P("seq", "dp"),
            P(("dp", "seq")),
            P("seq", "dp"),
            P("seq", "dp"),
            P(("dp", "seq")),
            P("seq", "dp"),
            P("seq", "dp"),
            P(("dp", "seq")),
            P("seq", "dp"),
            P("seq", "dp"),
            P(("dp", "seq")),
        ),
        check_vma=False,
    )
```

profile of v0, /device:TPU:19, one launch (start us, length us, event | category | flops | bytes accessed | tf_op | source)
XLA Modules:
  0.0 1264.9 jit_solution(12065567618159116973)
XLA Ops:
  9.9 31.6 %all-gather.8.cloned.1.call-done = bf16[1024,896]{1,0:T(8,128)(2,1)} async-done(((bf16[512,896]{1,0:T(8,128)(2,1)}), bf16[1024,896]{1,0:T(8,128)(2,1)}) %all-gather.8.cloned.1.call-update) | async-done | bytes 1835024 | tf_op jit(solution)/shard_map/all_gather | solution.py:59
  46.8 16.6 %all-gather.1 = bf16[16,1,896]{2,1,0:T(2,128)(2,1)S(1)} all-gather(bf16[1,1,896]{2,1,0:T(2,128)(2,1)S(1)} %reshape.660), channel_id=2, replica_groups=mesh['dp'=16,'seq'=2] {'dp'}, dimensions={0}, use_global_device_ids=true | all-gather | bytes 30464 | tf_op jit(solution)/shard_map/all_gather | solution.py:66
  64.7 127.0 %all-gather.10.cloned.1.call-done = bf16[1024,14336]{1,0:T(8,128)(2,1)} async-done(((bf16[1024,896]{1,0:T(8,128)(2,1)}), bf16[1024,14336]{1,0:T(8,128)(2,1)}) %all-gather.10.cloned.1.call-update) | async-done | bytes 29360144 | tf_op jit(solution)/shard_map/all_gather | solution.py:64
  210.8 28.5 %all-gather.12.cloned.1.call-done = bf16[1,1024,1024]{2,1,0:T(8,128)(2,1)} async-done(((bf16[1,512,1024]{2,1,0:T(8,128)(2,1)}), bf16[1,1024,1024]{2,1,0:T(8,128)(2,1)}) %all-gather.12.cloned.1.call-update) | async-done | bytes 2097168 | tf_op jit(solution)/shard_map/all_gather | solution.py:196
  242.1 32.3 %all-gather.14.cloned.1.call-done = bf16[1,1024,1024]{2,1,0:T(8,128)(2,1)} async-done(((bf16[1,512,1024]{2,1,0:T(8,128)(2,1)}), bf16[1,1024,1024]{2,1,0:T(8,128)(2,1)}) %all-gather.14.cloned.1.call-update) | async-done | bytes 2097168 | tf_op jit(solution)/shard_map/all_gather | solution.py:195
  279.4 54.1 %while.30 = (s32[]{:T(128)}, bf16[8,1,512,128]{2,3,1,0:T(8,128)(2,1)}, f32[8,1,2,512]{3,2,1,0:T(2,128)S(1)}, s32[8]{0:T(128)S(1)}, bf16[1,1024,1024]{1,2,0:T(8,1...) while((s32[]{:T(128)}, ...), condition=%wide.region_5.6_spmd, body=%wide.region_2.5_spmd.sunk | while | flops 277871616 | bytes 14975167 | solution.py:109
  356.8 104.5 %reduce-scatter.18.cloned.1.call-done = bf16[4096,64]{0,1:T(8,128)(2,1)} async-done(((bf16[4096,1024]{0,1:T(8,128)(2,1)}), bf16[4096,64]{0,1:T(8,128)(2,1)}) %reduce-scatter.18.cloned.1.call-update) | async-done | bytes 524304 | tf_op jit(solution)/shard_map/reduce_scatter | solution.py:296
  461.4 16.6 %reduce-scatter.20.cloned.1.call-done = bf16[2048,64]{0,1:T(8,128)(2,1)} async-done(((bf16[4096,64]{0,1:T(8,128)(2,1)}), bf16[2048,64]{0,1:T(8,128)(2,1)}) %reduce-scatter.20.cloned.1.call-update) | async-done | bytes 262160 | tf_op jit(solution)/shard_map/reduce_scatter | solution.py:307
  481.1 7.9 all_gather.34
  489.3 74.4 %all-gather.16.cloned.1.call-done = bf16[4096,1024]{0,1:T(8,128)(2,1)} async-done(((bf16[4096,64]{0,1:T(8,128)(2,1)}), bf16[4096,1024]{0,1:T(8,128)(2,1)}) %all-gather.16.cloned.1.call-update) | async-done | bytes 8388624 | tf_op jit(solution)/shard_map/all_gather | solution.py:65
  563.6 14.0 %fusion.108 = (bf16[4096]{0:T(1024)(128)(2,1)}, bf16[512,4096]{1,0:T(8,128)(2,1)S(1)}) fusion(f32[512,4096]{1,0:T(8,128)} %copy-done.44, f32[4096]{0:T(1024)S(1)} %bitcast.271, bf16[4096,1024]{0,1:T(8,128)(2,1)} %all-gather.16.cloned.1.call-done, f32[1024]{0:T(1024)S(1)} %bitcast.260, bf16[1,512,1024]{2,1,0:T(8,128)(2,1)} %param.26), kind=kOutput, calls=%fused_computation.175 | convolution fusion | flops 4342673408 | bytes 22048768 | tf_op jit(solution)/shard_map/nle,de->nld/dot_general | solution.py:46
  577.6 9.3 fusion.47
  594.9 89.9 %while.31 = (s32[]{:T(128)}, bf16[8,1,512,128]{2,3,1,0:T(8,128)(2,1)}, bf16[8,1,1024,128]{2,3,1,0:T(8,128)(2,1)}, bf16[8,1,1024,128]{2,3,1,0:T(8,128)(2,1)}, s32...) while((s32[]{:T(128)}, ...), condition=%wide.region_12.13_spmd, body=%wide.region_10.12_spmd.sunk | while | flops 684063744 | bytes 36597988 | solution.py:156
  687.8 28.6 %reduce-scatter.12.cloned.1.call-done = bf16[1,512,1024]{1,2,0:T(8,128)(2,1)} async-done(((bf16[1,1024,1024]{1,2,0:T(8,128)(2,1)}), bf16[1,512,1024]{1,2,0:T(8,128)(2,1)}) %reduce-scatter.12.cloned.1.call-update) | async-done | bytes 1048592 | tf_op jit(solution)/shard_map/reduce_scatter | solution.py:233
  716.4 34.1 %reduce-scatter.14.cloned.1.call-done = bf16[1,512,1024]{1,2,0:T(8,128)(2,1)} async-done(((bf16[1,1024,1024]{1,2,0:T(8,128)(2,1)}), bf16[1,512,1024]{1,2,0:T(8,128)(2,1)}) %reduce-scatter.14.cloned.1.call-update) | async-done | bytes 1048592 | tf_op jit(solution)/shard_map/reduce_scatter | solution.py:236
  762.3 13.8 %fusion.44 = (f32[1024]{0:T(1024)S(1)}, f32[1024]{0:T(1024)S(1)}, f32[1,512,1024]{2,1,0:T(8,128)}, bf16[1,512,1024]{2,1,0:T(8,128)(2,1)}) fusion(bf16[1,512,1024]{2,1,0:T(8,128)(2,1)S(1)} %copy-done.14, f32[1024]{0:T(1024)S(1)} %bitcast.285, f32[512,1024]{1,0:T(8,128)} %get-tuple-element.280, f32[1024]{0:T(1024)S(1)} %bitcast.287, ...), kind=kOutput, calls=%fused_computation.81 | convolution fusion | flops 4326946816 | bytes 30459904 | tf_op jit(solution)/shard_map/nld,de->nle/dot_general | solution.py:42
  776.2 7.9 psum.7
  784.2 8.6 multiply_select_fusion
  792.8 15.0 %scatter.14 = bf16[1024,14336]{1,0:T(8,128)(2,1)} pad(bf16[1024,6144]{1,0:T(8,128)(2,1)} %multiply_select_fusion, f32[]{:T(128)} %constant.203.clone.1), padding=0_0x0_8192 | pad | bytes 41943044 | tf_op jit(solution)/shard_map/scatter | solution.py:278
  807.9 9.6 select_dynamic-update-slice_fusion
  830.1 38.5 %copy.41 = bf16[1024,14336]{0,1:T(8,128)(2,1)} copy(bf16[1024,14336]{1,0:T(8,128)(2,1)} %convolution_dynamic-update-slice_fusion) | data formatting | bytes 58720256
  873.9 274.7 %reduce-scatter.22.cloned.1.call-done = bf16[896,1024]{1,0:T(8,128)(2,1)} async-done(((bf16[14336,1024]{1,0:T(8,128)(2,1)}), bf16[896,1024]{1,0:T(8,128)(2,1)}) %reduce-scatter.22.cloned.1.call-update) | async-done | bytes 1835024
  1160.2 59.0 %reduce-scatter.24.cloned.1.call-done = bf16[896,1]{1,0:T(8,128)(2,1)} async-done(((bf16[14336,1]{1,0:T(8,128)(2,1)}), bf16[896,1]{1,0:T(8,128)(2,1)}) %reduce-scatter.24.cloned.1.call-update) | async-done | bytes 1808
  1224.8 27.2 %reduce-scatter.16.cloned.1.call-done = bf16[512,896]{1,0:T(8,128)(2,1)} async-done(((bf16[1024,896]{1,0:T(8,128)(2,1)}), bf16[512,896]{1,0:T(8,128)(2,1)}) %reduce-scatter.16.cloned.1.call-update) | async-done | bytes 917520 | tf_op jit(solution)/shard_map/reduce_scatter | solution.py:304
  (375 shorter events, 257.8 us)
Async XLA Ops:
  7.2 34.2 %all-gather.8.cloned.1.call-start = ((), (), s32[]{:S(2)}) async-start(), calls=%async_computation.7 | async-start | bytes 2752512 | tf_op jit(solution)/shard_map/all_gather | solution.py:59
  9.8 53.6 %copy-start = (bf16[1,512,1024]{2,1,0:T(8,128)(2,1)S(1)}, bf16[1,512,1024]{2,1,0:T(8,128)(2,1)}, u32[]{:S(2)}) copy-start(bf16[1,512,1024]{2,1,0:T(8,128)(2,1)} %param.24) | copy-start | bytes 3145732
  9.8 181.9 %copy-start.20 = (bf16[1,1024]{1,0:T(2,128)(2,1)S(1)}, bf16[1,1024]{1,0:T(2,128)(2,1)}, u32[]{:S(2)}) copy-start(bf16[1,1024]{1,0:T(2,128)(2,1)} %param.25) | copy-start | bytes 6148
  9.8 181.9 %all-gather.10.cloned.1.call-start = ((), (), s32[]{:S(2)}) async-start(), calls=%async_computation.8 | async-start | bytes 31195136 | tf_op jit(solution)/shard_map/all_gather | solution.py:64
  41.4 197.9 %all-gather.12.cloned.1.call-start = ((), (), s32[]{:S(2)}) async-start(), calls=%async_computation.9 | async-start | bytes 3145728 | tf_op jit(solution)/shard_map/all_gather | solution.py:196
  63.6 133.7 %copy-start.26 = (f32[512]{0:T(512)}, f32[512]{0:T(512)S(1)}, u32[]{:S(2)}) copy-start(f32[512]{0:T(512)S(1)} %broadcast_multiply_fusion.1) | copy-start | bytes 6148
  64.0 133.2 %copy-start.24 = (f32[512]{0:T(512)}, f32[512]{0:T(512)S(1)}, u32[]{:S(2)}) copy-start(f32[512]{0:T(512)S(1)} %fusion.41) | copy-start | bytes 6148
  64.1 133.2 %copy-start.22 = (f32[512]{0:T(512)}, f32[512]{0:T(512)S(1)}, u32[]{:S(2)}) copy-start(f32[512]{0:T(512)S(1)} %fusion.86) | copy-start | bytes 6148
  197.3 141.2 %copy-start.33 = (f32[1,1024]{1,0:T(1,128)}, f32[1,1024]{1,0:T(1,128)S(1)}, u32[]{:S(2)}) copy-start(f32[1,1024]{1,0:T(1,128)S(1)} %get-tuple-element.273) | copy-start | bytes 12292
  206.1 68.4 %all-gather.14.cloned.1.call-start = ((), (), s32[]{:S(2)}) async-start(), calls=%async_computation.10 | async-start | bytes 3145728 | tf_op jit(solution)/shard_map/all_gather | solution.py:195
  208.9 252.5 %reduce-scatter.18.cloned.1.call-start = ((), (), s32[]{:S(2)}) async-start(), calls=%async_computation.15 | async-start | bytes 8912896 | tf_op jit(solution)/shard_map/reduce_scatter | solution.py:296
  356.8 121.2 %reduce-scatter.20.cloned.1.call-start = ((), (), s32[]{:S(2)}) async-start(), calls=%async_computation.16 | async-start | bytes 786432 | tf_op jit(solution)/shard_map/reduce_scatter | solution.py:307
  461.4 102.2 %all-gather.16.cloned.1.call-start = ((), (), s32[]{:S(2)}) async-start(), calls=%async_computation.11 | async-start | bytes 8912896 | tf_op jit(solution)/shard_map/all_gather | solution.py:65
  489.0 227.4 %reduce-scatter.12.cloned.1.call-start = ((), (), s32[]{:S(2)}) async-start(), calls=%async_computation.12 | async-start | bytes 3145728 | tf_op jit(solution)/shard_map/reduce_scatter | solution.py:233
  684.9 65.7 %reduce-scatter.14.cloned.1.call-start = ((), (), s32[]{:S(2)}) async-start(), calls=%async_computation.13 | async-start | bytes 3145728 | tf_op jit(solution)/shard_map/reduce_scatter | solution.py:236
  684.9 65.6 %copy-start.27 = (f32[512]{0:T(512)S(1)}, f32[512]{0:T(512)}, u32[]{:S(2)}) copy-start(f32[512]{0:T(512)} %copy-done.26) | copy-start | bytes 6148
  684.9 65.6 %copy-start.29 = (f32[1,1024]{1,0:T(1,128)S(1)}, f32[1,1024]{1,0:T(1,128)}, u32[]{:S(2)}) copy-start(f32[1,1024]{1,0:T(1,128)} %copy-done.28) | copy-start | bytes 12292
  685.6 463.0 %reduce-scatter.22.cloned.1.call-start = ((), (), s32[]{:S(2)}) async-start(), calls=%async_computation.17 | async-start | bytes 31195136
  868.6 350.6 %reduce-scatter.24.cloned.1.call-start = ((), (), s32[]{:S(2)}) async-start(), calls=%async_computation.18 | async-start | bytes 3899392
  873.7 378.3 %reduce-scatter.16.cloned.1.call-start = ((), (), s32[]{:S(2)}) async-start(), calls=%async_computation.14 | async-start | bytes 2752512 | tf_op jit(solution)/shard_map/reduce_scatter | solution.py:304
  1153.1 71.0 %copy-start.32 = (f32[448]{0:T(512)S(1)}, f32[448]{0:T(512)}, u32[]{:S(2)}) copy-start(f32[448]{0:T(512)} %param.29) | copy-start | bytes 5380
  1153.1 71.0 %copy-start.39 = (f32[448]{0:T(512)S(1)}, f32[448]{0:T(512)}, u32[]{:S(2)}) copy-start(f32[448]{0:T(512)} %param.35) | copy-start | bytes 5380
  1153.1 71.0 %copy-start.40 = (f32[448]{0:T(512)S(1)}, f32[448]{0:T(512)}, u32[]{:S(2)}) copy-start(f32[448]{0:T(512)} %param.32) | copy-start | bytes 5380
  1153.1 98.9 %copy-start.8 = (f32[512,896]{1,0:T(8,128)S(1)}, f32[512,896]{1,0:T(8,128)}, u32[]{:S(2)}) copy-start(f32[512,896]{1,0:T(8,128)} %param.27) | copy-start | bytes 5505028
  (33 other events, 254.5 us)
Sparse Core Ops, SparseCore 0:
  10.2 31.2 all-gather.7
  43.0 148.6 all-gather.9
  206.2 33.0 all-gather.11
  241.3 33.1 all-gather.13
  356.9 104.3 reduce-scatter.17
  463.5 14.4 reduce-scatter.19
  489.1 74.4 all-gather.15
  685.0 31.3 reduce-scatter.11
  718.7 31.8 reduce-scatter.13
  868.7 279.8 reduce-scatter.21
  1153.0 66.2 reduce-scatter.23
  1221.9 30.0 reduce-scatter.15
where the time goes:
time: 1270 us; the launch traced here: 1260 us
  waiting for transfers between devices  839 us (66%)
  matrix products  159 us (13%)
  local copies, waits for them, and re-layouts  150 us (12%)
  other arithmetic  47.2 us (4%)
  blocking collectives  39.9 us (3%)
  between operations  16.3 us (1%)
    unnamed x14, waiting for transfers between devices  335 us
    all_gather x1, waiting for transfers between devices, gather_weights(): lax.all_gather(seq_parts[0], 'dp', axis=1, tiled=True)  127 us
    reduce_scatter x1, waiting for transfers between devices, local(): lax.psum_scatter(grad_down.astype(jnp.bfloat16), 'dp', scatter_dimension=...  105 us
    all_gather x1, waiting for transfers between devices, gather_weights(): lax.all_gather(seq_parts[1], 'dp', axis=1, tiled=True)  74.4 us
    unnamed x106, local copies, waits for them, and re-layouts  54.7 us
    dynamic_slice x56, local copies, waits for them, and re-layouts, split_heads(): piece = lax.dynamic_slice_in_dim(values, lane_start, lane_count, 2)  38.9 us
    dot_general x4, matrix products, dense_back(): jnp.einsum('nle,de->nld', gradients, matrix, preferred_element_type=jnp.f...  35.1 us
    reduce_scatter x1, waiting for transfers between devices, local(): lax.psum_scatter(value_terms.astype(jnp.bfloat16), 'seq', scatter_dimensi...  34.1 us
  transfers between devices with their start and end apart: 12, of which 12 were waited for; matrix products, arithmetic and copies ran while one was open for 2% of the time, Pallas kernels for 0%

commit v1 on v0

--- a/solution.py
+++ b/solution.py
@@ -3,6 +3,8 @@
 import jax
 import jax.numpy as jnp
 from jax import lax
+from jax.experimental import pallas as pl
+from jax.experimental.pallas import tpu as pltpu
 from jax.sharding import PartitionSpec as P
 
 D = 1024
@@ -157,7 +159,7 @@
     return (join_heads(query_terms), join_heads(key_terms), join_heads(value_terms))
 
 
-def local(
+def local_general(
     hidden_in,
     condition,
     cotangent,
@@ -339,9 +341,1514 @@
     )
 
 
+MESH = pl.DeviceIdType.MESH
+WIDE = 896
+LOW = 6 * D
+KEPT = 4 * D + FF
+PLANES = 4
+HALF = D // 2
+TALL = HALF + 16
+SUBS = 3
+SUB_ROWS = TALL // SUBS
+FF_PART = FF // 2
+DP = 16
+
+
+def place():
+    dp = lax.axis_index("dp")
+    y = lax.axis_index("seq")
+    return (dp // 4, lax.rem(dp // 2, 2), lax.rem(dp, 2), y)
+
+
+def device_at(z, x, c, y):
+    return ((z * 2 + x) * 2 + c, y)
+
+
+def neighbours():
+    z, x, c, y = place()
+    return {
+        "x": device_at(z, 1 - x, c, y),
+        "y": device_at(z, x, c, 1 - y),
+        "up": device_at(jnp.minimum(z + 1, PLANES - 1), x, c, y),
+        "down": device_at(jnp.maximum(z - 1, 0), x, c, y),
+        "core": device_at(z, x, 1 - c, y),
+        "swap": device_at(z, x, 1 - c, 1 - y),
+    }
+
+
+def repeat(count, body):
+    def step(at, carried):
+        body(at)
+        return carried
+
+    lax.fori_loop(0, count, step, 0)
+
+
+def greet_all():
+    barrier = pltpu.get_barrier_semaphore()
+    here = lax.axis_index("dp") * 2 + lax.axis_index("seq")
+
+    def signal(at):
+        there = lax.rem(here + at + 1, 2 * DP)
+        pl.semaphore_signal(
+            barrier, inc=1, device_id=(there // 2, lax.rem(there, 2)), device_id_type=MESH
+        )
+
+    repeat(2 * DP - 1, signal)
+    pl.semaphore_wait(barrier, 2 * DP - 1)
+
+
+class Broad:
+    height, width, subs, split = SUB_ROWS, WIDE, SUBS, 96
+    first, source_column = 0, 0
+
+    @staticmethod
+    def holds(zs, xs, cs):
+        return (zs * 2 + xs) * 2 + cs >= 7
+
+    @staticmethod
+    def view(whole, zs, xs, ys, cs, sub, start=0, rows=SUB_ROWS):
+        column = jnp.maximum(((zs * 2 + xs) * 2 + cs) * WIDE - LOW, 128)
+        row = pl.multiple_of(sub * SUB_ROWS + start, 16)
+        return whole.at[ys, pl.ds(row, rows), pl.ds(pl.multiple_of(column, 128), WIDE)]
+
+
+class Narrow:
+    height, width, subs, split = TALL, 128, 1, 272
+    first, source_column = 16 * SUBS, WIDE - 128
+
+    @staticmethod
+    def holds(zs, xs, cs):
+        return (zs * 2 + xs) * 2 + cs == 6
+
+    @staticmethod
+    def view(whole, zs, xs, ys, cs, sub, start=0, rows=TALL):
+        return whole.at[ys, pl.ds(start, rows), pl.ds(0, 128)]
+
+
+class Down:
+    height, width, subs, split = 64, FF_PART, 1, 32
+    first, source_column = 16 * SUBS + 16, 0
+
+    @staticmethod
+    def holds(zs, xs, cs):
+        return zs >= 0
+
+    @staticmethod
+    def view(whole, zs, xs, ys, cs, sub, start=0, rows=64):
+        row = pl.multiple_of(((zs * 2 + xs) * 2 + cs) * 64 + start, 32)
+        return whole.at[pl.ds(row, rows), pl.ds(pl.multiple_of(ys * FF_PART, 128), FF_PART)]
+
+
+SLOTS = 16 * SUBS + 32
+RELATIONS = ("own", "x", "y", "xy")
+HOPS = {"own": 0, "x": 1, "y": 1, "xy": 2}
+
+
+def by_plane(z, table):
+    picked = table[PLANES - 1]
+    for plane in range(PLANES - 2, -1, -1):
+        picked = jnp.where(z == plane, table[plane], picked)
+    return picked
+
+
+def forward_block(what, refs, kind, zs, relation, sub, sems, valid):
+    whole, mine = refs
+    send_sem, recv_sem, core_sem = sems
+    z, x, c, y = place()
+    near = neighbours()
+    xs = 1 - x if "x" in relation else x
+    ys = 1 - y if "y" in relation else y
+    slot = kind.first + ((zs * 2 + xs) * 2 + ys) * kind.subs + sub
+    full, half = recv_sem.at[slot, 0], recv_sem.at[slot, 1]
+    parts = ((0, kind.height), (0, kind.split), (kind.split, kind.height - kind.split))
+
+    def copy(part, index, arrival, key, source=None, cs=None):
+        target = kind.view(whole, zs, xs, ys, c if cs is None else cs, sub, *parts[part])
+        return pltpu.make_async_remote_copy(
+            src_ref=target if source is None else source,
+            dst_ref=target,
+            send_sem=send_sem.at[slot, index],
+            recv_sem=arrival,
+            device_id=near[key],
+            device_id_type=MESH,
+        )
+
+    if what == "core":
+
+        @pl.when(valid & kind.holds(zs, xs, 1 - c))
+        def _():
+            copy(0, 4, core_sem.at[slot], "core", cs=1 - c).wait_recv()
+
+        return
+    valid = valid & kind.holds(zs, xs, c)
+    if what == "tick":
+        arrived = valid & (zs != z) if relation == "own" else valid
+
+        @pl.when(arrived)
+        def _():
+            if relation == "xy":
+                copy(1, 0, full, "x").wait_recv()
+                copy(2, 0, half, "x").wait_recv()
+            else:
+                copy(0, 0, full, "x").wait_recv()
+
+    def act(descriptor):
+        if what == "tick":
+            descriptor.start()
+        else:
+            descriptor.wait_send()
+
+    def spread(source, upward, downward):
+        @pl.when(upward)
+        def _():
+            act(copy(0, 0, full, "up", source))
+
+        @pl.when(downward)
+        def _():
+            act(copy(0, 1, full, "down", source))
+
+        act(copy(0, 2, full, "x", source))
+        act(copy(0, 3, full, "y", source))
+        act(copy(0, 4, core_sem.at[slot], "core", source))
+
+    if relation == "own":
+
+        @pl.when(valid & (zs == z))
+        def _():
+            source = mine.at[
+                pl.ds(pl.multiple_of(sub * kind.height, 16), kind.height),
+                pl.ds(kind.source_column, kind.width),
+            ]
+            spread(source, z < PLANES - 1, z > 0)
+
+        @pl.when(valid & (zs != z))
+        def _():
+            spread(None, (zs < z) & (z < PLANES - 1), (zs > z) & (z > 0))
+
+        return
+
+    @pl.when(valid)
+    def _():
+        if relation == "x":
+            act(copy(1, 3, full, "y"))
+        if relation == "y":
+            act(copy(2, 2, half, "x"))
+        act(copy(0, 4, core_sem.at[slot], "core"))
+
+
+def forward_step(what, refs, plan, sems, at):
+    z = place()[0]
+    for kind, order, after in plan:
+        for position in range(len(order[0])):
+            zs = by_plane(z, [row[position] for row in order])
+            for relation in RELATIONS:
+                sub = at
+                if what == "tick":
+                    sub = at - (after + position + HOPS[relation])
+                forward_block(
+                    what,
+                    refs[kind.__name__],
+                    kind,
+                    zs,
+                    relation,
+                    jnp.clip(sub, 0, kind.subs - 1),
+                    sems,
+                    (sub >= 0) & (sub < kind.subs),
+                )
+
+
+NEAR_LOW = ((1, 2), (1, 2), (2, 1), (2, 1))
+ONLY_ONE = ((1,),) * PLANES
+ONLY_LAST = ((3,),) * PLANES
+NEAR = ((0, 1, 2, 3), (1, 0, 2, 3), (2, 3, 1, 0), (3, 2, 1, 0))
+PLAN_LOW = ((Broad, NEAR_LOW, 0), (Narrow, ONLY_ONE, 0))
+PLAN_UP = ((Broad, ONLY_LAST, 3),)
+PLAN_DOWN = ((Down, NEAR, 6),)
+PLAN_ALL = PLAN_LOW + PLAN_UP + PLAN_DOWN
+EARLY_STEPS = 6
+LATE_STEPS = 12
+
+
+BF16 = jnp.bfloat16
+F32 = jnp.float32
+PLAIN = (((1,), (0,)), ((), ()))
+BOTH_LAST = (((1,), (1,)), ((), ()))
+BOTH_FIRST = (((0,), (0,)), ((), ()))
+LANES = 128
+PAIRS = HEADS // 2
+TOKENS_HERE = 512
+
+
+def multiply(left, right, dims=PLAIN):
+    return lax.dot_general(left, right, dims, preferred_element_type=F32)
+
+
+def two_heads(block):
+    lanes = lax.broadcasted_iota(jnp.int32, block.shape, 1)
+    zero = jnp.zeros_like(block)
+    return (jnp.where(lanes < HEAD_DIM, block, zero), jnp.where(lanes < HEAD_DIM, zero, block))
+
+
+def attend_pair(pair, queries, keys, values, mixed, log_totals):
+    columns = pl.ds(pl.multiple_of(pair * LANES, LANES), LANES)
+    key_block = keys[:, columns]
+    value_flat = values[:, columns].T
+    parts = []
+    for head, query_block in enumerate(two_heads(queries[:, columns])):
+        scores = multiply(key_block, query_block, BOTH_LAST)
+        largest = jnp.max(scores, axis=0, keepdims=True)
+        weights = jnp.exp((scores - largest) * HEAD_DIM**-0.5)
+        total = jnp.sum(weights, axis=0, keepdims=True)
+        parts.append(multiply(value_flat, weights.astype(BF16)) * (1.0 / total))
+        log_totals[2 * pair + head] = largest * HEAD_DIM**-0.5 + jnp.log(total)
+    joined = jnp.concatenate([parts[0][:HEAD_DIM], parts[1][HEAD_DIM:]], axis=0)
+    mixed[:, columns] = joined.T.astype(BF16)
+
+
+def normalize(values):
+    center = values - jnp.mean(values, axis=-1, keepdims=True)
+    return center * lax.rsqrt(jnp.mean(center * center, axis=-1, keepdims=True) + norm_eps)
+
+
+def from_weights(left, whole, start, width):
+    columns = pl.ds(pl.multiple_of(start, LANES), width)
+    return multiply(left[:, :HALF], whole[0, :HALF, columns]) + multiply(
+        left[:, HALF:], whole[1, :HALF, columns]
+    )
+
+
+def bias_of(whole, start, width):
+    columns = pl.ds(pl.multiple_of(start, LANES), width)
+    both = whole[0, HALF:TALL, columns].astype(F32) + whole[1, HALF:TALL, columns].astype(F32)
+    return both[:1]
+
+
+def forward_kernel(
+    low_in,
+    low_down,
+    hidden_in,
+    cotangent,
+    condition,
+    ada_bias,
+    whole_in,
+    whole_down,
+    hidden,
+    grad_out,
+    cond_all,
+    modulation,
+    input_one,
+    queries,
+    keys,
+    values,
+    mixed,
+    log_totals,
+    attn_out,
+    middle,
+    input_two,
+    upward,
+    grad_branch,
+    gate_grad,
+    block_out,
+    own_in,
+    own_down,
+    ada_weights,
+    ada_part,
+    mod_parts,
+    up_stage,
+    wide,
+    active,
+    out_stage,
+    send_sem,
+    recv_sem,
+    core_sem,
+    local_sem,
+    cond_send,
+    cond_recv,
+    mod_send,
+    mod_recv,
+    swap_sem,
+    pair_sem,
+    up_sem,
+):
+    z, x, c, y = place()
+    dp = (z * 2 + x) * 2 + c
+    near = neighbours()
+    sems = (send_sem, recv_sem, core_sem)
+    refs = {"Broad": (own_in, low_in), "Narrow": (own_in, low_in), "Down": (own_down, low_down)}
+    at_home = c == y
+
+    def remote(source, target, sent, arrived, device):
+        return pltpu.make_async_remote_copy(
+            src_ref=source,
+            dst_ref=target,
+            send_sem=sent,
+            recv_sem=arrived,
+            device_id=device,
+            device_id_type=MESH,
+        )
+
+    broad = pltpu.make_async_copy(
+        low_in,
+        own_in.at[y, :, pl.ds(pl.multiple_of(jnp.maximum(dp, 7) * WIDE - LOW, LANES), WIDE)],
+        local_sem.at[0],
+    )
+    narrow = pltpu.make_async_copy(
+        low_in.at[:, pl.ds(WIDE - 128, 128)], own_in.at[y, :, pl.ds(0, 128)], local_sem.at[0]
+    )
+    down = pltpu.make_async_copy(
+        low_down,
+        own_down.at[
+            pl.ds(pl.multiple_of(dp * 64, 64), 64),
+            pl.ds(pl.multiple_of(y * FF_PART, LANES), FF_PART),
+        ],
+        local_sem.at[1],
+    )
+    ada = pltpu.make_async_copy(low_in.at[pl.ds(0, HALF)], ada_weights, local_sem.at[2])
+    ada.start()
+    down.start()
+
+    @pl.when(dp >= 7)
+    def _():
+        broad.start()
+
+    @pl.when(dp == 6)
+    def _():
+        narrow.start()
+
+    greet_all()
+
+    cond_all[dp] = condition[...]
+
+    def cond_copy(at):
+        there = lax.rem(dp + at + 1, DP)
+        return remote(
+            condition, cond_all.at[dp], cond_send.at[at], cond_recv.at[dp], (there, y)
+        )
+
+    repeat(DP - 1, lambda at: cond_copy(at).start())
+
+    swaps = []
+    for index, (source, target) in enumerate(((hidden_in, hidden), (cotangent, grad_out))):
+        swaps.append(
+            (
+                pltpu.make_async_copy(source, target, swap_sem.at[index, 0]),
+                remote(
+                    source, target, swap_sem.at[index, 1], swap_sem.at[index, 2], near["swap"]
+                ),
+            )
+        )
+
+    def trade(index):
+        @pl.when(at_home)
+        def _():
+            swaps[index][0].start()
+
+        @pl.when(jnp.logical_not(at_home))
+        def _():
+            swaps[index][1].start()
+
+    def traded(index):
+        @pl.when(at_home)
+        def _():
+            swaps[index][0].wait()
+
+        @pl.when(jnp.logical_not(at_home))
+        def _():
+            swaps[index][1].wait()
+
+    trade(0)
+    repeat(2, lambda at: forward_step("tick", refs, PLAN_LOW, sems, at))
+
+    def cond_arrived(at):
+        there = lax.rem(dp + at + 1, DP)
+        remote(
+            condition, cond_all.at[there], cond_send.at[at], cond_recv.at[there], (there, y)
+        ).wait_recv()
+
+    repeat(DP - 1, cond_arrived)
+    raw = jnp.concatenate([cond_all[index] for index in range(DP)], axis=0)
+    active[...] = (raw / (1.0 + jnp.exp(-raw))).astype(BF16)
+    ada.wait()
+    partial = (
+        multiply(
+            active[:, pl.ds(pl.multiple_of(y * HALF, LANES), HALF)],
+            ada_weights[...],
+        )
+        + ada_bias[...]
+    )
+    for index in range(DP):
+        ada_part[index] = partial[index : index + 1]
+
+    def mod_target(at):
+        latent, core = at // 2, lax.rem(at, 2)
+        return (latent // 2 * 2 + core, lax.rem(latent, 2))
+
+    def mod_copy(at):
+        return remote(
+            ada_part.at[at // 2],
+            mod_parts.at[dp * 2 + y],
+            mod_send.at[at],
+            mod_recv.at[dp * 2 + y],
+            mod_target(at),
+        )
+
+    def elsewhere(at):
+        there = mod_target(at)
+        return (there[0] != dp) | (there[1] != y)
+
+    @pl.when(dp < 7)
+    def _():
+        def send(at):
+            @pl.when(elsewhere(at))
+            def _():
+                mod_copy(at).start()
+
+            @pl.when(jnp.logical_not(elsewhere(at)))
+            def _():
+                mod_parts[dp * 2 + y] = ada_part[at // 2]
+
+        repeat(2 * DP, send)
+
+    forward_step("tick", refs, PLAN_LOW, sems, 2)
+    trade(1)
+    traded(0)
+
+    def mod_arrived(at):
+        @pl.when(at != dp * 2 + y)
+        def _():
+            remote(
+                ada_part.at[0], mod_parts.at[at], mod_send.at[0], mod_recv.at[at], near["x"]
+            ).wait_recv()
+
+    repeat(14, mod_arrived)
+    for index in range(7):
+        modulation[:, index * WIDE : (index + 1) * WIDE] = (
+            mod_parts[2 * index] + mod_parts[2 * index + 1]
+        )
+
+    def vector(index):
+        return modulation[:, index * D : (index + 1) * D]
+
+    def shape_one(at):
+        rows = pl.ds(pl.multiple_of(at * 128, 128), 128)
+        normed = normalize(hidden[rows].astype(F32))
+        input_one[rows] = (normed * (1.0 + vector(1)) + vector(0)).astype(BF16)
+
+    repeat(4, shape_one)
+
+    repeat(
+        EARLY_STEPS - 3,
+        lambda at: forward_step("tick", refs, PLAN_LOW + PLAN_UP, sems, at + 3),
+    )
+    repeat(SUBS, lambda at: forward_step("core", refs, PLAN_LOW, sems, at))
+
+    @pl.when(dp >= 7)
+    def _():
+        broad.wait()
+
+    @pl.when(dp == 6)
+    def _():
+        narrow.wait()
+
+    def project(at):
+        columns = pl.ds(pl.multiple_of(at * 256, LANES), 256)
+        keys[:HALF, columns] = from_weights(input_one, own_in, D + at * 256, 256).astype(BF16)
+        values[:HALF, columns] = (
+            from_weights(input_one, own_in, 2 * D + at * 256, 256)
+            + bias_of(own_in, D + at * 256, 256)
+        ).astype(BF16)
+
+    repeat(D // 256, project)
+    mates = [
+        remote(
+            one.at[:HALF], one.at[HALF:], pair_sem.at[index, 0], pair_sem.at[index, 1], near["core"]
+        )
+        for index, one in enumerate((keys, values))
+    ]
+    for mate in mates:
+        mate.start()
+
+    def project_queries(at):
+        columns = pl.ds(pl.multiple_of(at * 256, LANES), 256)
+        queries[:, columns] = (
+            from_weights(input_one, own_in, at * 256, 256) + bias_of(own_in, at * 256, 256)
+        ).astype(BF16)
+
+    repeat(D // 256, project_queries)
+    for mate in mates:
+        mate.wait()
+
+    def attention(pair):
+        attend_pair(pair, queries, keys, values, mixed, log_totals)
+
+        @pl.when(lax.rem(pair, 4) == 3)
+        def _():
+            forward_step("tick", refs, PLAN_UP + PLAN_DOWN, sems, EARLY_STEPS + pair // 4)
+
+    repeat(PAIRS, attention)
+
+    def project_out(at):
+        columns = pl.ds(pl.multiple_of(at * 256, LANES), 256)
+        attn_out[:, columns] = from_weights(mixed, own_in, 3 * D + at * 256, 256) + bias_of(
+            own_in, 2 * D + at * 256, 256
+        )
+
+    repeat(D // 256, project_out)
+
+    def shape_two(at):
+        rows = pl.ds(pl.multiple_of(at * 128, 128), 128)
+        mid = hidden[rows].astype(F32) + vector(2) * attn_out[rows]
+        middle[rows] = mid
+        input_two[rows] = (normalize(mid) * (1.0 + vector(4)) + vector(3)).astype(BF16)
+
+    repeat(4, shape_two)
+    repeat(SUBS, lambda at: forward_step("core", refs, PLAN_UP, sems, at))
+    whole_copies = [
+        pltpu.make_async_copy(
+            own_in.at[half, pl.ds(0, HALF)],
+            whole_in.at[pl.ds(half * HALF, HALF)],
+            local_sem.at[3 + half],
+        )
+        for half in range(2)
+    ]
+    for whole_copy in whole_copies:
+        whole_copy.start()
+    tile = 512
+
+    def up_copy(at, slot):
+        return pltpu.make_async_copy(
+            up_stage.at[slot],
+            upward.at[:, pl.ds(pl.multiple_of(at * tile, LANES), tile)],
+            up_sem.at[slot],
+        )
+
+    def widen(at):
+        slot = lax.rem(at, 2)
+
+        @pl.when(at >= 2)
+        def _():
+            up_copy(at - 2, slot).wait()
+
+        for side in range(2):
+            start = at * tile + side * 256
+            value = from_weights(input_two, own_in, 4 * D + start, 256) + bias_of(
+                own_in, 3 * D + start, 256
+            )
+            up_stage[slot, :, side * 256 : (side + 1) * 256] = value
+            inner = math.sqrt(2.0 / math.pi) * (value + 0.044715 * (value * value * value))
+            wide[:, pl.ds(pl.multiple_of(start, LANES), 256)] = (
+                0.5 * value * (1.0 + jnp.tanh(inner))
+            ).astype(BF16)
+        up_copy(at, slot).start()
+
+        @pl.when(lax.rem(at, 2) == 1)
+        def _():
+            forward_step("tick", refs, PLAN_DOWN, sems, EARLY_STEPS + 2 + at // 2)
+
+    repeat(FF // tile, widen)
+    for at in (FF // tile - 2, FF // tile - 1):
+        up_copy(at, at % 2).wait()
+    forward_step("core", refs, PLAN_DOWN, sems, 0)
+    down.wait()
+    down_copy = pltpu.make_async_copy(own_down, whole_down, local_sem.at[5])
+    down_copy.start()
+    traded(1)
+
+    def narrow_down(at):
+        columns = pl.ds(pl.multiple_of(at * 256, LANES), 256)
+        value = bias_of(own_in, 7 * D + at * 256, 256)
+        for side in range(2):
+            value += multiply(
+                wide[:, side * FF_PART : (side + 1) * FF_PART],
+                own_down[columns, side * FF_PART : (side + 1) * FF_PART],
+                BOTH_LAST,
+            )
+        gate = modulation[:, pl.ds(pl.multiple_of(5 * D + at * 256, LANES), 256)]
+        out_stage[:, columns] = (middle[:, columns] + gate * value).astype(BF16)
+        towards = grad_out[:, columns].astype(F32)
+        gate_grad[:, columns] = jnp.sum(towards * value, axis=0, keepdims=True)
+        grad_branch[:, columns] = (towards * gate).astype(BF16)
+
+    repeat(D // 256, narrow_down)
+    home = pltpu.make_async_copy(out_stage, block_out, swap_sem.at[2, 0])
+    away = remote(out_stage, block_out, swap_sem.at[2, 1], swap_sem.at[2, 2], near["swap"])
+
+    @pl.when(at_home)
+    def _():
+        home.start()
+        home.wait()
+
+    @pl.when(jnp.logical_not(at_home))
+    def _():
+        away.start()
+        away.wait()
+
+    repeat(SUBS, lambda at: forward_step("drain", refs, PLAN_ALL, sems, at))
+    repeat(DP - 1, lambda at: cond_copy(at).wait_send())
+
+    @pl.when(dp < 7)
+    def _():
+        def sent(at):
+            @pl.when(elsewhere(at))
+            def _():
+                mod_copy(at).wait_send()
+
+        repeat(2 * DP, sent)
+
+    for whole_copy in whole_copies:
+        whole_copy.wait()
+    down_copy.wait()
+
+
+def run_forward(low_in, low_down, hidden_in, cotangent, condition, ada_bias):
+    shape = jax.ShapeDtypeStruct
+    rows = TOKENS_HERE
+    outs = [
+        (shape((D, KEPT), BF16), pl.ANY),
+        (shape((D, FF), BF16), pl.ANY),
+        (shape((rows, D), BF16), pltpu.VMEM),
+        (shape((rows, D), BF16), pltpu.VMEM),
+        (shape((DP, 1, D), F32), pltpu.VMEM),
+        (shape((1, 7 * WIDE), F32), pltpu.VMEM),
+        (shape((rows, D), BF16), pltpu.VMEM),
+        (shape((rows, D), BF16), pltpu.VMEM),
+        (shape((2 * rows, D), BF16), pltpu.VMEM),
+        (shape((2 * rows, D), BF16), pltpu.VMEM),
+        (shape((rows, D), BF16), pltpu.VMEM),
+        (shape((HEADS, 1, rows), F32), pltpu.VMEM),
+        (shape((rows, D), F32), pltpu.VMEM),
+        (shape((rows, D), F32), pltpu.VMEM),
+        (shape((rows, D), BF16), pltpu.VMEM),
+        (shape((rows, FF), F32), pl.ANY),
+        (shape((rows, D), BF16), pltpu.VMEM),
+        (shape((1, D), F32), pltpu.VMEM),
+        (shape((rows, D), BF16), pl.ANY),
+    ]
+    dma = pltpu.SemaphoreType.DMA
+    return pl.pallas_call(
+        forward_kernel,
+        out_shape=[one for one, _ in outs],
+        in_specs=[pl.BlockSpec(memory_space=pl.ANY)] * 4
+        + [pl.BlockSpec(memory_space=pltpu.VMEM)] * 2,
+        out_specs=[pl.BlockSpec(memory_space=where) for _, where in outs],
+        scratch_shapes=[
+            pltpu.VMEM((2, TALL, KEPT), BF16),
+            pltpu.VMEM((D, FF), BF16),
+            pltpu.VMEM((HALF, WIDE), BF16),
+            pltpu.VMEM((DP, 1, WIDE), F32),
+            pltpu.VMEM((14, 1, WIDE), F32),
+            pltpu.VMEM((2, rows, 512), F32),
+            pltpu.VMEM((rows, FF), BF16),
+            pltpu.VMEM((DP, D), BF16),
+            pltpu.VMEM((rows, D), BF16),
+            dma((SLOTS, 5)),
+            dma((SLOTS, 2)),
+            dma((SLOTS,)),
+            dma((6,)),
+            dma((DP,)),
+            dma((DP,)),
+            dma((2 * DP,)),
+            dma((14,)),
+            dma((3, 3)),
+            dma((2, 2)),
+            dma((2,)),
+        ],
+        compiler_params=pltpu.CompilerParams(
+            collective_id=0, has_side_effects=True, vmem_limit_bytes=62 * 2**20
+        ),
+        name="forward",
+    )(low_in, low_down, hidden_in, cotangent, condition, ada_bias)
+
+
+GRAD_SUBS = 4
+GRAD_ROWS = HALF // GRAD_SUBS
+
+
+class BroadGrad:
+    height, width, subs, source_column = GRAD_ROWS, WIDE, GRAD_SUBS, 0
+
+    @staticmethod
+    def holds(zs, xs, cs):
+        return (zs * 2 + xs) * 2 + cs >= 7
+
+    @staticmethod
+    def corner(zs, xs, ys, cs, sub):
+        column = jnp.maximum(((zs * 2 + xs) * 2 + cs) * WIDE - LOW, 128)
+        return (
+            pl.multiple_of(ys * HALF + sub * GRAD_ROWS, GRAD_ROWS),
+            pl.multiple_of(column, 128),
+        )
+
+
+class NarrowGrad:
+    height, width, subs, source_column = HALF, 128, 1, WIDE - 128
+
+    @staticmethod
+    def holds(zs, xs, cs):
+        return (zs * 2 + xs) * 2 + cs == 6
+
+    @staticmethod
+    def corner(zs, xs, ys, cs, sub):
+        return (pl.multiple_of(ys * HALF, HALF), 0)
+
+
+def reduce_block(what, refs, kind, zs, plane_at, planes, relation, sub, sems, valid):
+    grads, first_column, owned, buffers = refs
+    from_core, from_x, from_y, from_low, from_high, half_a, half_b = buffers
+    send_sem, recv_sem = sems
+    z, x, c, y = place()
+    near = neighbours()
+    xs = 1 - x if "x" in relation else x
+    ys = 1 - y if "y" in relation else y
+    flat = plane_at * kind.subs + sub
+    count = planes * kind.subs
+    kin = RELATIONS.index(relation)
+    slot = kin * count + flat
+    rows, half_rows = kind.height, kind.height // 2
+
+    def remote(source, target, index, arrival, key):
+        return pltpu.make_async_remote_copy(
+            src_ref=source,
+            dst_ref=target,
+            send_sem=send_sem.at[slot, index],
+            recv_sem=recv_sem.at[arrival, flat],
+            device_id=near[key],
+            device_id_type=MESH,
+        )
+
+    def share(cs):
+        row, column = kind.corner(zs, xs, ys, cs, sub)
+        column = jnp.clip(column - first_column, 0, grads.shape[1] - kind.width)
+        return (pl.ds(row, rows), pl.ds(pl.multiple_of(column, 128), kind.width))
+
+    total = from_core.at[slot]
+    across = remote(grads.at[share(1 - c)], total, 2, kin, "core")
+    other = valid & kind.holds(zs, xs, 1 - c)
+    if what == "across":
+        pl.when(other)(across.start)
+        return
+    if what == "drain":
+        pl.when(other)(across.wait_send)
+    valid = valid & kind.holds(zs, xs, c)
+    part_a = from_core.at[slot, pl.ds(0, half_rows)]
+    part_b = from_core.at[slot, pl.ds(half_rows, half_rows)]
+    if relation == "xy":
+        sends = [
+            (valid, remote(part_a, half_a.at[flat], 0, 4, "y")),
+            (valid, remote(part_b, half_b.at[flat], 1, 5, "x")),
+        ]
+    elif relation == "x":
+        sends = [(valid, remote(total, from_x.at[flat], 0, 6, "x"))]
+    elif relation == "y":
+        sends = [(valid, remote(total, from_y.at[flat], 0, 7, "y"))]
+    else:
+        sends = [
+            (valid & (z < zs), remote(total, from_low.at[flat], 0, 8, "up")),
+            (valid & (z > zs), remote(total, from_high.at[flat], 1, 9, "down")),
+        ]
+    if what == "drain":
+        for condition, descriptor in sends:
+            pl.when(condition)(descriptor.wait_send)
+        return
+
+    @pl.when(valid)
+    def _():
+        remote(total, total, 2, kin, "core").wait_recv()
+        value = from_core[slot].astype(F32) + grads[share(c)].astype(F32)
+        if relation == "xy":
+            from_core[slot] = value.astype(BF16)
+        elif relation == "x":
+            remote(half_a.at[flat], half_a.at[flat], 0, 4, "y").wait_recv()
+            from_core[slot, pl.ds(half_rows, half_rows)] = value[half_rows:].astype(BF16)
+            from_core[slot, pl.ds(0, half_rows)] = (
+                value[:half_rows] + half_a[flat].astype(F32)
+            ).astype(BF16)
+        elif relation == "y":
+            remote(half_b.at[flat], half_b.at[flat], 1, 5, "x").wait_recv()
+            from_core[slot, pl.ds(0, half_rows)] = value[:half_rows].astype(BF16)
+            from_core[slot, pl.ds(half_rows, half_rows)] = (
+                value[half_rows:] + half_b[flat].astype(F32)
+            ).astype(BF16)
+        else:
+            remote(from_x.at[flat], from_x.at[flat], 0, 6, "x").wait_recv()
+            remote(from_y.at[flat], from_y.at[flat], 0, 7, "y").wait_recv()
+            value += from_x[flat].astype(F32) + from_y[flat].astype(F32)
+
+            @pl.when((z <= zs) & (z > 0))
+            def _():
+                remote(from_low.at[flat], from_low.at[flat], 0, 8, "up").wait_recv()
+
+            @pl.when((z >= zs) & (z < PLANES - 1))
+            def _():
+                remote(from_high.at[flat], from_high.at[flat], 1, 9, "down").wait_recv()
+
+            def low():
+                return jnp.where(z > 0, from_low[flat].astype(F32), 0.0)
+
+            def high():
+                return jnp.where(z < PLANES - 1, from_high[flat].astype(F32), 0.0)
+
+            @pl.when(z < zs)
+            def _():
+                from_core[slot] = (value + low()).astype(BF16)
+
+            @pl.when(z > zs)
+            def _():
+                from_core[slot] = (value + high()).astype(BF16)
+
+            @pl.when(z == zs)
+            def _():
+                owned[
+                    pl.ds(pl.multiple_of(sub * rows, rows), rows),
+                    pl.ds(kind.source_column, kind.width),
+                ] = value + low() + high()
+
+    for condition, descriptor in sends:
+        pl.when(condition)(descriptor.start)
+
+
+def reduce_step(what, refs, plan, sems, at):
+    z = place()[0]
+    for kind, planes in plan:
+        name = kind.__name__
+        for plane_at, zs in enumerate(planes):
+            for relation in ("xy", "x", "y", "own"):
+                sub = at
+                if what == "tick":
+                    depth = 0
+                    if relation == "own":
+                        depth = by_plane(
+                            z,
+                            [
+                                place_z
+                                if place_z < zs
+                                else max(place_z, 3 - place_z)
+                                if place_z == zs
+                                else 3 - place_z
+                                for place_z in range(PLANES)
+                            ],
+                        )
+                    sub = at - (2 - HOPS[relation] + depth)
+                reduce_block(
+                    what,
+                    refs[name],
+                    kind,
+                    zs,
+                    plane_at,
+                    len(planes),
+                    relation,
+                    jnp.clip(sub, 0, kind.subs - 1),
+                    sems[name],
+                    (sub >= 0) & (sub < kind.subs),
+                )
+
+
+def landing(kind, planes):
+    count = planes * kind.subs
+    full = pltpu.VMEM((count, kind.height, kind.width), BF16)
+    half = pltpu.VMEM((count, kind.height // 2, kind.width), BF16)
+    return [pltpu.VMEM((4 * count, kind.height, kind.width), BF16)] + [full] * 4 + [half] * 2
+
+
+def landing_signals(kind, planes):
+    count = planes * kind.subs
+    return [pltpu.SemaphoreType.DMA((4 * count, 3)), pltpu.SemaphoreType.DMA((10, count))]
+
+
+def greet_near():
+    z, x, c, y = place()
+    near = neighbours()
+    barrier = pltpu.get_barrier_semaphore()
+    for key in ("x", "y", "core"):
+        pl.semaphore_signal(barrier, inc=1, device_id=near[key], device_id_type=MESH)
+
+    @pl.when(z < PLANES - 1)
+    def _():
+        pl.semaphore_signal(barrier, inc=1, device_id=near["up"], device_id_type=MESH)
+
+    @pl.when(z > 0)
+    def _():
+        pl.semaphore_signal(barrier, inc=1, device_id=near["down"], device_id_type=MESH)
+
+    middle = (z > 0) & (z < PLANES - 1)
+
+    @pl.when(middle)
+    def _():
+        pl.semaphore_wait(barrier, 5)
+
+    @pl.when(jnp.logical_not(middle))
+    def _():
+        pl.semaphore_wait(barrier, 4)
+
+
+REDUCE_HIGH = ((BroadGrad, (3,)),)
+REDUCE_LOW = ((BroadGrad, (1, 2)), (NarrowGrad, (1,)))
+HIGH_STEPS = GRAD_SUBS + 5
+LOW_STEPS = GRAD_SUBS + 5
+HIGH_FIRST = FF // 8
+
+
+def attend_back(
+    pair, queries, keys, values, mixed, grad_mixed, log_totals, grad_query, grad_key, grad_value
+):
+    columns = pl.ds(pl.multiple_of(pair * LANES, LANES), LANES)
+    key_block = keys[:, columns]
+    value_block = values[:, columns]
+    key_flat = key_block.T
+    key_sum, value_sum = None, None
+    step = 256
+    for part in range(TOKENS_HERE // step):
+        rows = pl.ds(part * step, step)
+        grad_block = grad_mixed[rows, columns]
+        product = (grad_block.astype(F32) * mixed[rows, columns].astype(F32)).T
+        query_parts = []
+        heads = zip(two_heads(queries[rows, columns]), two_heads(grad_block))
+        for head, (query_head, grad_head) in enumerate(heads):
+            scores = multiply(key_block, query_head, BOTH_LAST)
+            weights = jnp.exp(scores * HEAD_DIM**-0.5 - log_totals[2 * pair + head, :, rows])
+            grad_weights = multiply(value_block, grad_head, BOTH_LAST)
+            inner = jnp.sum(
+                product[HEAD_DIM * head : HEAD_DIM * (head + 1)], axis=0, keepdims=True
+            )
+            grad_scores = (weights * (grad_weights - inner)).astype(BF16)
+            value_term = multiply(weights.astype(BF16), grad_head)
+            key_term = multiply(grad_scores, query_head)
+            value_sum = value_term if value_sum is None else value_sum + value_term
+            key_sum = key_term if key_sum is None else key_sum + key_term
+            query_parts.append(multiply(key_flat, grad_scores))
+        joined = jnp.concatenate([query_parts[0][:HEAD_DIM], query_parts[1][HEAD_DIM:]], axis=0)
+        grad_query[rows, columns] = (joined * HEAD_DIM**-0.5).T.astype(BF16)
+    grad_key[:, columns] = (key_sum * HEAD_DIM**-0.5).astype(BF16)
+    grad_value[:, columns] = value_sum.astype(BF16)
+
+
+def backward_kernel(
+    queries,
+    keys,
+    values,
+    mixed,
+    grad_mixed,
+    log_totals,
+    grads,
+    grad_query,
+    grad_key,
+    grad_value,
+    owned,
+    key_all,
+    value_all,
+    key_mate,
+    value_mate,
+    mate_sem,
+    *scratch,
+):
+    dp = lax.axis_index("dp")
+    near = neighbours()
+    refs = {"BroadGrad": (grads, 4 * D, owned, scratch[:7])}
+    sems = {"BroadGrad": scratch[7:9]}
+    greet_near()
+    repeat(GRAD_SUBS, lambda at: reduce_step("across", refs, REDUCE_HIGH, sems, at))
+
+    @pl.when(dp < 12)
+    def _():
+        owned[...] = jnp.zeros_like(owned)
+
+    def mates(pair):
+        columns = pl.ds(pl.multiple_of(pair * LANES, LANES), LANES)
+        return [
+            pltpu.make_async_remote_copy(
+                src_ref=source.at[HALF:, columns],
+                dst_ref=target.at[:, columns],
+                send_sem=mate_sem.at[pair, 2 * index],
+                recv_sem=mate_sem.at[pair, 2 * index + 1],
+                device_id=near["core"],
+                device_id_type=MESH,
+            )
+            for index, (source, target) in enumerate(((key_all, key_mate), (value_all, value_mate)))
+        ]
+
+    def attention(pair):
+        reduce_step("tick", refs, REDUCE_HIGH, sems, pair)
+        attend_back(
+            pair,
+            queries,
+            keys,
+            values,
+            mixed,
+            grad_mixed,
+            log_totals,
+            grad_query,
+            key_all,
+            value_all,
+        )
+        for mate in mates(pair):
+            mate.start()
+
+    repeat(PAIRS, attention)
+    for source, target, total, index in (
+        (key_all, key_mate, grad_key, 0),
+        (value_all, value_mate, grad_value, 1),
+    ):
+        repeat(PAIRS, lambda pair: mates(pair)[index].wait())
+        total[...] = (source[:HALF].astype(F32) + target[...].astype(F32)).astype(BF16)
+    repeat(
+        HIGH_STEPS - PAIRS, lambda at: reduce_step("tick", refs, REDUCE_HIGH, sems, at + PAIRS)
+    )
+    repeat(GRAD_SUBS, lambda at: reduce_step("drain", refs, REDUCE_HIGH, sems, at))
+
+
+def run_backward(queries, keys, values, mixed, grad_mixed, log_totals, grads):
+    shape = jax.ShapeDtypeStruct
+    rows = TOKENS_HERE
+    vmem = pl.BlockSpec(memory_space=pltpu.VMEM)
+    return pl.pallas_call(
+        backward_kernel,
+        out_shape=[shape((rows, D), BF16)] * 3 + [shape((HALF, WIDE), F32)],
+        in_specs=[vmem] * 7,
+        out_specs=[vmem] * 4,
+        scratch_shapes=[pltpu.VMEM((2 * rows, D), BF16)] * 2
+        + [pltpu.VMEM((rows, D), BF16)] * 2
+        + [pltpu.SemaphoreType.DMA((PAIRS, 4))]
+        + landing(BroadGrad, 1)
+        + landing_signals(BroadGrad, 1),
+        compiler_params=pltpu.CompilerParams(
+            collective_id=1, has_side_effects=True, vmem_limit_bytes=60 * 2**20
+        ),
+        cost_estimate=pl.CostEstimate(
+            flops=5 * 2 * 512 * 1024 * 1024 * 2, bytes_accessed=60 * 2**20, transcendentals=2**23
+        ),
+        name="backward",
+    )(queries, keys, values, mixed, grad_mixed, log_totals, grads)
+
+
+VECTOR = 17 * WIDE
+
+
+def finish_kernel(
+    grad_qkv,
+    grad_out_proj,
+    grad_up,
+    low_in,
+    active_rows,
+    condition,
+    sums,
+    input_grad,
+    owned_high,
+    owned,
+    cond_grad,
+    bias_parts,
+    ada_bias_grad,
+    input_swapped,
+    grads,
+    ada_weights,
+    sum_mate,
+    sum_pieces,
+    ada_in,
+    cond_piece,
+    cond_in,
+    local_sem,
+    mate_sem,
+    piece_send,
+    ada_recv,
+    bias_recv,
+    cond_send,
+    cond_recv,
+    swap_sem,
+    *scratch,
+):
+    z, x, c, y = place()
+    dp = (z * 2 + x) * 2 + c
+    near = neighbours()
+    refs = {
+        "BroadGrad": (grads, 0, owned, scratch[0:7]),
+        "NarrowGrad": (grads, 0, owned, scratch[7:14]),
+    }
+    sems = {"BroadGrad": scratch[14:16], "NarrowGrad": scratch[16:18]}
+    at_home = c == y
+
+    def remote(source, target, sent, arrived, device):
+        return pltpu.make_async_remote_copy(
+            src_ref=source,
+            dst_ref=target,
+            send_sem=sent,
+            recv_sem=arrived,
+            device_id=device,
+            device_id_type=MESH,
+        )
+
+    loads = [
+        pltpu.make_async_copy(grad_qkv, grads.at[:, : 3 * D], local_sem.at[0]),
+        pltpu.make_async_copy(grad_out_proj, grads.at[:, 3 * D : 4 * D], local_sem.at[1]),
+        pltpu.make_async_copy(
+            grad_up.at[:, :HIGH_FIRST], grads.at[:, 4 * D : 4 * D + HIGH_FIRST], local_sem.at[2]
+        ),
+        pltpu.make_async_copy(low_in.at[pl.ds(0, HALF)], ada_weights, local_sem.at[3]),
+    ]
+    for load in loads:
+        load.start()
+    owned[...] = owned_high[...]
+    greet_all()
+    mate = remote(sums, sum_mate, mate_sem.at[0], mate_sem.at[1], near["core"])
+    mate.start()
+    away = remote(input_grad, input_swapped, swap_sem.at[0], swap_sem.at[1], near["swap"])
+
+    for load in loads[:3]:
+        load.wait()
+    repeat(GRAD_SUBS, lambda at: reduce_step("across", refs, REDUCE_LOW, sems, at))
+
+    mate.wait()
+    for index in range(17):
+        columns = slice(index * WIDE, (index + 1) * WIDE)
+        piece = sums[:, columns] + sum_mate[:, columns]
+        if index < 7:
+            piece = piece.astype(BF16).astype(F32)
+        sum_pieces[index] = piece
+    latent = (z * 2 + x) * 2 + y
+
+    def piece_target(at):
+        return jnp.where(at < 7, at, at - 1)
+
+    def piece_copy(at, target, arrived):
+        return remote(
+            sum_pieces.at[at], target, piece_send.at[at], arrived, (piece_target(at), c)
+        )
+
+    def each_piece(act, keep):
+        def go(at):
+            mine = (piece_target(at) == dp) & (y == c)
+
+            @pl.when(jnp.logical_not(mine) & (at < 7))
+            def _():
+                act(piece_copy(at, ada_in.at[latent], ada_recv.at[latent]))
+
+            @pl.when(jnp.logical_not(mine) & (at >= 7))
+            def _():
+                act(piece_copy(at, bias_parts.at[latent], bias_recv.at[latent]))
+
+            if keep:
+
+                @pl.when(mine & (at < 7))
+                def _():
+                    ada_in[latent] = sum_pieces[at]
+
+                @pl.when(mine & (at >= 7))
+                def _():
+                    bias_parts[latent] = sum_pieces[at]
+
+        repeat(17, go)
+
+    each_piece(lambda copy: copy.start(), True)
+    repeat(3, lambda at: reduce_step("tick", refs, REDUCE_LOW, sems, at))
+
+    @pl.when(jnp.logical_not(at_home))
+    def _():
+        away.start()
+
+    def from_latent(at, target, arrived):
+        mine = (at // 2 == z * 2 + x) & (lax.rem(at, 2) == y) & (c == y)
+
+        @pl.when(jnp.logical_not(mine))
+        def _():
+            remote(
+                sum_pieces.at[0], target.at[at], piece_send.at[0], arrived.at[at], near["x"]
+            ).wait_recv()
+
+    loads[3].wait()
+
+    @pl.when(dp < 7)
+    def _():
+        repeat(DP, lambda at: from_latent(at, ada_in, ada_recv))
+        gathered = jnp.concatenate([ada_in[index] for index in range(DP)], axis=0)
+        ada_bias_grad[...] = jnp.sum(gathered, axis=0, keepdims=True)
+        narrow = gathered.astype(BF16)
+        owned[...] += multiply(active_rows[...], narrow, BOTH_FIRST)
+        part = multiply(narrow, ada_weights[...], BOTH_LAST)
+        for index in range(DP):
+            cond_piece[index] = part[index : index + 1]
+
+    @pl.when(dp >= 7)
+    def _():
+        ada_bias_grad[...] = jnp.zeros_like(ada_bias_grad)
+
+    def cond_copy(at):
+        return remote(
+            cond_piece.at[at // 2],
+            cond_in.at[dp * 2 + y],
+            cond_send.at[at],
+            cond_recv.at[dp * 2 + y],
+            (at // 2, lax.rem(at, 2)),
+        )
+
+    def each_cond(act, keep):
+        def go(at):
+            mine = at == dp * 2 + y
+
+            @pl.when(jnp.logical_not(mine))
+            def _():
+                act(cond_copy(at))
+
+            if keep:
+
+                @pl.when(mine)
+                def _():
+                    cond_in[dp * 2 + y] = cond_piece[at // 2]
+
+        repeat(2 * DP, go)
+
+    @pl.when(dp < 7)
+    def _():
+        each_cond(lambda copy: copy.start(), True)
+
+    repeat(LOW_STEPS - 3, lambda at: reduce_step("tick", refs, REDUCE_LOW, sems, at + 3))
+
+    def cond_arrived(at):
+        @pl.when(at != dp * 2 + y)
+        def _():
+            remote(
+                cond_piece.at[0], cond_in.at[at], cond_send.at[0], cond_recv.at[at], near["x"]
+            ).wait_recv()
+
+    repeat(14, cond_arrived)
+    sides = []
+    for side in range(2):
+        total = cond_in[side]
+        for index in range(1, 7):
+            total = total + cond_in[2 * index + side]
+        sides.append(total)
+    value = condition[...]
+    logistic = 1.0 / (1.0 + jnp.exp(-value))
+    cond_grad[...] = jnp.concatenate(sides, axis=1) * (
+        logistic * (1.0 + value * (1.0 - logistic))
+    )
+
+    @pl.when(dp >= 6)
+    def _():
+        repeat(DP, lambda at: from_latent(at, bias_parts, bias_recv))
+
+    @pl.when(dp < 6)
+    def _():
+        bias_parts[...] = jnp.zeros_like(bias_parts)
+
+    @pl.when(jnp.logical_not(at_home))
+    def _():
+        away.wait()
+
+    each_piece(lambda copy: copy.wait_send(), False)
+
+    @pl.when(dp < 7)
+    def _():
+        each_cond(lambda copy: copy.wait_send(), False)
+
+    repeat(GRAD_SUBS, lambda at: reduce_step("drain", refs, REDUCE_LOW, sems, at))
+
+
+def run_finish(
+    grad_qkv, grad_out_proj, grad_up, low_in, active_rows, condition, sums, input_grad, owned_high
+):
+    shape = jax.ShapeDtypeStruct
+    dma = pltpu.SemaphoreType.DMA
+    vmem = pl.BlockSpec(memory_space=pltpu.VMEM)
+    hbm = pl.BlockSpec(memory_space=pl.ANY)
+    return pl.pallas_call(
+        finish_kernel,
+        out_shape=[
+            shape((HALF, WIDE), F32),
+            shape((1, D), F32),
+            shape((DP, 1, WIDE), F32),
+            shape((1, WIDE), F32),
+            shape((TOKENS_HERE, D), BF16),
+        ],
+        in_specs=[hbm] * 4 + [vmem] * 3 + [hbm, vmem],
+        out_specs=[vmem] * 4 + [hbm],
+        scratch_shapes=[
+            pltpu.VMEM((D, 4 * D + HIGH_FIRST), BF16),
+            pltpu.VMEM((HALF, WIDE), BF16),
+            pltpu.VMEM((1, VECTOR), F32),
+            pltpu.VMEM((17, 1, WIDE), F32),
+            pltpu.VMEM((DP, 1, WIDE), F32),
+            pltpu.VMEM((DP, 1, HALF), F32),
+            pltpu.VMEM((14, 1, HALF), F32),
+            dma((4,)),
+            dma((2,)),
+            dma((17,)),
+            dma((DP,)),
+            dma((DP,)),
+            dma((2 * DP,)),
+            dma((14,)),
+            dma((2,)),
+        ]
+        + landing(BroadGrad, 2)
+        + landing(NarrowGrad, 1)
+        + landing_signals(BroadGrad, 2)
+        + landing_signals(NarrowGrad, 1),
+        compiler_params=pltpu.CompilerParams(
+            collective_id=2, has_side_effects=True, vmem_limit_bytes=60 * 2**20
+        ),
+        name="finish",
+    )(grad_qkv, grad_out_proj, grad_up, low_in, active_rows, condition, sums, input_grad, owned_high)
+
+
+def local(
+    hidden_in,
+    condition,
+    cotangent,
+    weights_in,
+    weights_down,
+    biases,
+    moment_in,
+    moment_down,
+    moment_bias,
+    square_in,
+    square_down,
+    square_bias,
+):
+    dp = lax.axis_index("dp")
+    y = lax.axis_index("seq")
+    side = WIDE // 2
+    bias_row = jnp.pad(biases.astype(BF16)[None], ((0, 15), (0, side)))
+    bias_row = jnp.where(y == 0, bias_row, jnp.roll(bias_row, side, axis=1))
+    low_in = jnp.concatenate([weights_in.astype(BF16), bias_row], axis=0)
+    cond_float = condition.astype(F32)
+    (
+        whole_in,
+        whole_down,
+        hidden,
+        grad_out,
+        cond_all,
+        modulation,
+        input_one,
+        queries,
+        keys,
+        values,
+        mixed,
+        log_totals,
+        attn_out,
+        middle,
+        input_two,
+        upward,
+        grad_branch,
+        gate_two_grad,
+        block_out,
+    ) = run_forward(
+        low_in,
+        weights_down.astype(BF16).T,
+        hidden_in[0],
+        cotangent[0],
+        cond_float,
+        bias_row[:1].astype(F32),
+    )
+    grad_out = grad_out.astype(F32)
+    pieces = [modulation[:, part * D : (part + 1) * D] for part in range(6)]
+    shift_one, scale_one, gate_one, shift_two, scale_two, gate_two = pieces
+
+    def back_through(gradients, start, width):
+        return lax.dot_general(
+            gradients,
+            whole_in[:, start : start + width],
+            BOTH_LAST,
+            preferred_element_type=F32,
+        )
+
+    def outer(left, right):
+        return lax.dot_general(left, right, BOTH_FIRST, preferred_element_type=F32)
+
+    def down_rows(total):
+        return jnp.sum(total.astype(F32), axis=0, keepdims=True)
+
+    activated, gelu_pull = jax.vjp(lambda inner: jax.nn.gelu(inner, approximate=True), upward)
+    grad_down = outer(activated.astype(BF16), grad_branch)
+    grad_act = jnp.dot(grad_branch, whole_down, preferred_element_type=F32)
+    grad_upward = gelu_pull(grad_act)[0].astype(BF16)
+    grad_up = outer(input_two, grad_upward).astype(BF16)
+    grad_input_two = back_through(grad_upward, 4 * D, FF)
+    normed_two, norm_pull_two = jax.vjp(layer_norm, middle)
+    shift_two_grad = down_rows(grad_input_two)
+    scale_two_grad = down_rows(grad_input_two * normed_two)
+    grad_middle = grad_out + norm_pull_two(grad_input_two * (1.0 + scale_two))[0]
+    grad_attn = (grad_middle * gate_one).astype(BF16)
+    gate_one_grad = down_rows(grad_middle * attn_out)
+    grad_out_proj = outer(mixed, grad_attn).astype(BF16)
+    grad_mixed = back_through(grad_attn, 3 * D, D).astype(BF16)
+    down_sum = lax.psum_scatter(
+        grad_down.astype(BF16), "dp", scatter_dimension=1, tiled=True
+    )
+    grad_query, grad_key, grad_value, owned_high = run_backward(
+        queries, keys, values, mixed, grad_mixed, log_totals, grad_up
+    )
+    grad_qkv = jnp.concatenate([grad_query, grad_key, grad_value], axis=-1)
+    grad_proj_qkv = outer(input_one, grad_qkv).astype(BF16)
+    grad_input_one = back_through(grad_qkv, 0, 3 * D)
+    normed_one, norm_pull_one = jax.vjp(layer_norm, hidden.astype(F32))
+    shift_one_grad = down_rows(grad_input_one)
+    scale_one_grad = down_rows(grad_input_one * normed_one)
+    input_grad = grad_middle + norm_pull_one(grad_input_one * (1.0 + scale_one))[0]
+    sums = jnp.concatenate(
+        [
+            shift_one_grad,
+            scale_one_grad,
+            gate_one_grad,
+            shift_two_grad,
+            scale_two_grad,
+            gate_two_grad,
+            jnp.zeros((1, WIDE), F32),
+            down_rows(grad_query),
+            down_rows(grad_value),
+            down_rows(grad_attn),
+            down_rows(grad_upward),
+            down_rows(grad_branch),
+        ],
+        axis=-1,
+    )
+    active_rows = lax.dynamic_slice_in_dim(
+        jax.nn.silu(cond_all[:, 0]).astype(BF16), y * HALF, HALF, 1
+    )
+    owned_in, cond_grad, bias_parts, ada_bias_grad, input_swapped = run_finish(
+        grad_proj_qkv,
+        grad_out_proj,
+        grad_up,
+        low_in,
+        active_rows,
+        cond_float,
+        sums,
+        input_grad.astype(BF16),
+        owned_high,
+    )
+    at_home = lax.rem(dp, 2) == y
+    input_grad = jnp.where(at_home, input_grad, input_swapped.astype(F32))
+    owned_down = lax.psum_scatter(down_sum, "seq", scatter_dimension=0, tiled=True).astype(F32)
+    owned_bias = jnp.sum(bias_parts[:, 0], axis=0) + ada_bias_grad[0]
+    owned_bias = lax.dynamic_slice_in_dim(owned_bias, y * side, side, 0)
+    moments_in, squares_in, master_in = adamw_step(
+        weights_in, moment_in, square_in, owned_in, rate_in
+    )
+    moments_down, squares_down, master_down = adamw_step(
+        weights_down, moment_down, square_down, owned_down, rate_down
+    )
+    moments_bias, squares_bias, master_bias = adamw_step(
+        biases, moment_bias, square_bias, owned_bias, rate_bias
+    )
+    return (
+        block_out[None],
+        input_grad[None],
+        cond_grad,
+        moments_in,
+        moments_down,
+        moments_bias,
+        squares_in,
+        squares_down,
+        squares_bias,
+        master_in,
+        master_down,
+        master_bias,
+        master_in.astype(BF16),
+        master_down.astype(BF16),
+        master_bias.astype(BF16),
+    )
+
+
 def solution(mesh):
     return jax.shard_map(
-        local,
+        local if dict(mesh.shape) == {"dp": 16, "seq": 2} else local_general,
         mesh=mesh,
         in_specs=(
             P("dp", "seq", None),

time: 1270 us -> 493 us (0.39)
  waiting for transfers between devices: 839 us -> 9.07 us
  Pallas kernels: 0 us -> 365 us
  local copies, waits for them, and re-layouts: 150 us -> 9.81 us
  matrix products: 159 us -> 59.5 us
  blocking collectives: 39.9 us -> 0 us
  other arithmetic: 47.2 us -> 26 us
    pallas_call x0 -> x3, Pallas kernels: none -> 365 us  [the longest x1 185 us: run_forward(): pl.pallas_call(forward_kernel, out_shape=[one for one, _ in outs], in_spe...]
    unnamed x14 -> x2, waiting for transfers between devices: 335 us -> 0.03 us
    all_gather x5 -> x0, waiting for transfers between devices: 294 us -> none  [the longest x1 127 us: gather_weights(): lax.all_gather(seq_parts[0], 'dp', axis=1, tiled=True)]
    reduce_scatter x5 -> x2, waiting for transfers between devices: 211 us -> 9.04 us  [the longest x1 9.04 us: local(): lax.psum_scatter(down_sum, 'seq', scatter_dimension=0, tiled=True)]
    dot_general x70 -> x8, matrix products: 159 us -> 59.5 us  [the longest x4 24.3 us: outer(): return lax.dot_general(left, right, BOTH_FIRST, preferred_element_type=F32)]
    dynamic_slice x72 -> x0, local copies, waits for them, and re-layouts: 48.3 us -> none  [the longest x56 38.9 us: split_heads(): piece = lax.dynamic_slice_in_dim(values, lane_start, lane_count, 2)]
    unnamed x106 -> x80, local copies, waits for them, and re-layouts: 54.7 us -> 9.71 us
    all_gather x2 -> x0, blocking collectives: 24.5 us -> none  [the longest x1 16.6 us: gather_weights(): lax.all_gather(seq_parts[2].reshape(1, -1), 'dp', axis=1, tiled=True)]
  transfers between devices with their start and end apart: 12 -> 2, of which waited for: 12 -> 1; matrix products, arithmetic and copies ran while one was open for 2% -> 14% of each run, Pallas kernels for 0% -> 37%
where the time goes in v1:
time: 493 us; the launch traced here: 484 us
  Pallas kernels  365 us (74%)
  matrix products  59.5 us (12%)
  other arithmetic  26 us (5%)
  between operations  14.6 us (3%)
  local copies, waits for them, and re-layouts  9.81 us (2%)
  waiting for transfers between devices  9.07 us (2%)
    pallas_call x1, Pallas kernels, run_forward(): pl.pallas_call(forward_kernel, out_shape=[one for one, _ in outs], in_spe...  185 us
    pallas_call x1, Pallas kernels, run_backward(): pl.pallas_call(backward_kernel, out_shape=[shape((rows, D), BF16)] * 3 +...  102 us
    pallas_call x1, Pallas kernels, run_finish(): pl.pallas_call(finish_kernel, out_shape=[shape((HALF, WIDE), F32), shape(...  77.2 us
    dot_general x4, matrix products, outer(): return lax.dot_general(left, right, BOTH_FIRST, preferred_element_type=F32)  24.3 us
    dot_general x3, matrix products, back_through(): lax.dot_general(gradients, whole_in[:, start:start + width], BOTH_LAST, p...  20.3 us
    dot_general x1, matrix products, local(): grad_act = jnp.dot(grad_branch, whole_down, preferred_element_type=F32)  14.9 us
  transfers between devices with their start and end apart: 2, of which 1 were waited for; matrix products, arithmetic and copies ran while one was open for 14% of the time, Pallas kernels for 37%

profile of v1, /device:TPU:19, one launch (start us, length us, event | category | flops | bytes accessed | tf_op | source)
XLA Modules:
  0.0 483.6 jit_solution(16247586653285639236)
XLA Ops:
  7.9 1.3 convert_element_type.86.condition
  9.9 1.8 convert_bitcast_fusion.low_down
  11.7 1.6 convert_element_type.83
  13.3 1.0 pad_maximum_fusion.low_in
  14.3 185.3 %forward.1 = (bf16[1024,8192]{1,0:T(8,128)(2,1)}, bf16[1024,4096]{1,0:T(8,128)(2,1)}, bf16[512,1024]{1,0:T(8,128)(2,1)}, bf16[512,1024]{1,0:T(8,128)(2,1)}, f32[...) custom-call(bf16[528,896]{1,0:T(8,128)(2,1)} %pad_maximum_fusion.low, ...), custom_call_target="tpu_custom_call" | custom-call | tf_op jit(solution)/shard_map/forward/pallas_call | solution.py:1029
  199.6 9.5 %convolution_convert_fusion = bf16[4096,1024]{0,1:T(8,128)(2,1)} fusion(bf16[512,1024]{1,0:T(8,128)(2,1)} %get-tuple-element.45, f32[512,4096]{1,0:T(8,128)} %get-tuple-element.47), kind=kOutput, calls=%fused_computation.13 | convolution fusion | flops 4318035968 | bytes 17825792 | tf_op jit(solution)/shard_map/dot_general | solution.py:1753
  209.1 1.5 copy-done.1
  210.9 14.9 %convert_reduce_fusion = (f32[4096]{0:T(1024)S(1)}, bf16[512,4096]{1,0:T(8,128)(2,1)}) fusion(f32[512,4096]{1,0:T(8,128)} %get-tuple-element.47, bf16[512,1024]{1,0:T(8,128)(2,1)S(1)} %copy-done.13, bf16[1024,4096]{1,0:T(8,128)(2,1)} %get-tuple-element.46), kind=kOutput, calls=%fused_computation.10 | convolution fusion | flops 4341100544 | bytes 22036480 | tf_op jit(solution)/shard_map/dot_general | solution.py:1760
  227.4 9.7 %multiply_reduce_fusion = (f32[1024]{0:T(1024)S(1)}, f32[512]{0:T(512)S(1)}, f32[1024]{0:T(1024)S(1)}, f32[512,1024]{1,0:T(8,128)S(1)}) fusion(f32[512,1024]{1,0:T(8,128)S(1)} %copy-done.1, f32[512]{0:T(512)S(1)} %fusion.32, f32[512]{0:T(512)S(1)} %broadcast_multiply_fusion.1, f32[1024]{0:T(1024)S(1)} %bitcast.48, bf16[512,4096]{1,0:T(8,128)(2,1)} %get-tuple-element.92, ...), kind=kOutput, calls=%fused_computation.41 | convolution fusion | flops 4299159040 | bytes 16795648 | tf_op jit(solution)/shard_map/dot_general | solution.py:1745
  239.0 4.5 fusion.26.grad_mixed
  243.5 6.7 %convolution_convert_fusion.1.grads.grad_up = bf16[1024,4096]{1,0:T(8,128)(2,1)} fusion(bf16[512,1024]{1,0:T(8,128)(2,1)S(1)} %copy-done.30, bf16[512,4096]{1,0:T(8,128)(2,1)S(1)} %copy-done.31), kind=kOutput, calls=%fused_computation.14 | convolution fusion | flops 4299161600 | bytes 13631488 | tf_op jit(solution)/shard_map/dot_general | solution.py:1753
  250.2 102.0 %backward.1 = (bf16[512,1024]{1,0:T(8,128)(2,1)}, bf16[512,1024]{1,0:T(8,128)(2,1)}, bf16[512,1024]{1,0:T(8,128)(2,1)}, f32[512,896]{1,0:T(8,128)}) custom-call(bf16[512,1024]{1,0:T(8,128)(2,1)} %get-tuple-element.51.queries, bf16[1024,1024]{1,0:T(8,128)(2,1)} %get-tuple-element.52.keys, bf16[1024,1024]{1,0:T(8,128)(2,1)} %get-tuple-element.53.values, ...), custom_call_target="tpu_custom_call" | custom-call | flops 10737418240 | bytes 62914560 | tf_op jit(solution)/shard_map/backward/pallas_call | solution.py:1404
  352.3 1.4 constant_dynamic-update-slice_fusion.2
  354.2 0.9 copy-done.3
  356.2 6.1 %fusion.20 = (f32[512]{0:T(512)S(1)}, f32[1024]{0:T(1024)S(1)}, f32[1024]{0:T(1024)S(1)}, f32[512,1024]{1,0:T(8,128)S(1)}) fusion(bf16[512,1024]{1,0:T(8,128)(2,1)S(1)} %copy-done.3, f32[512]{0:T(512)S(1)} %broadcast_multiply_fusion, f32[1024]{0:T(1024)S(1)} %bitcast.45, f32[512]{0:T(512)S(1)} %fusion.33, ...), kind=kOutput, calls=%fused_computation.33 | convolution fusion | flops 3225941504 | bytes 12601344 | tf_op jit(solution)/shard_map/dot_general | solution.py:1745
  363.9 1.7 fusion.30
  367.2 2.6 convolution_convert_fusion.3.grad_out_proj
  369.8 5.4 %convolution_convert_fusion.2.grad_qkv = bf16[1024,3072]{1,0:T(8,128)(2,1)} fusion(bf16[512,1024]{1,0:T(8,128)(2,1)S(1)} %copy-done.28, bf16[512,3072]{1,0:T(8,128)(2,1)S(1)} %constant_dynamic-update-slice_fusion), kind=kOutput, calls=%fused_computation.17 | convolution fusion | flops 3224371200 | bytes 10485760 | tf_op jit(solution)/shard_map/dot_general | solution.py:1753
  375.2 77.2 %finish.1 = (f32[512,896]{1,0:T(8,128)}, f32[1,1024]{1,0:T(1,128)}, f32[16,1,896]{2,1,0:T(1,128)}, f32[1,896]{1,0:T(1,128)}, bf16[512,1024]{1,0:T(8,128)(2,1)}) custom-call(bf16[1024,3072]{1,0:T(8,128)(2,1)} %convolution_convert_fusion.2.grad_qkv, bf16[1024,1024]{1,0:T(8,128)(2,1)} %convolution_convert_fusion.3.grad_out_proj, ...), custom_call_target="tpu_custom_call" | custom-call | tf_op jit(solution)/shard_map/finish/pallas_call | solution.py:1652
  454.9 3.9 select_bitcast_fusion
  459.7 3.8 fusion.42
  463.5 9.0 %reduce-scatter.5.cloned.1.call-done = bf16[2048,64]{0,1:T(8,128)(2,1)} async-done(((bf16[4096,64]{0,1:T(8,128)(2,1)}), bf16[2048,64]{0,1:T(8,128)(2,1)}) %reduce-scatter.5.cloned.1.call-update) | async-done | bytes 262160 | tf_op jit(solution)/shard_map/reduce_scatter | solution.py:1818
  472.5 2.4 fusion.40
  474.9 1.0 copy.45
  (110 shorter events, 13.6 us)
Async XLA Ops:
  7.2 447.6 %reduce-scatter.3.cloned.1.call-start = ((), (), s32[]{:S(2)}) async-start(), calls=%async_computation.2 | async-start | bytes 8912896 | tf_op jit(solution)/shard_map/reduce_scatter | solution.py:1772
  209.1 1.8 copy-start.13
  209.1 263.4 %reduce-scatter.5.cloned.1.call-start = ((), (), s32[]{:S(2)}) async-start(), calls=%async_computation.3 | async-start | bytes 786432 | tf_op jit(solution)/shard_map/reduce_scatter | solution.py:1818
  227.4 9.8 %copy-start.2 = (f32[512,1024]{1,0:T(8,128)S(1)}, f32[512,1024]{1,0:T(8,128)}, u32[]{:S(2)}) copy-start(f32[512,1024]{1,0:T(8,128)} %get-tuple-element.50) | copy-start | bytes 6291460
  239.0 4.5 copy-start.17
  239.0 4.5 copy-start.30
  239.0 4.5 copy-start.31
  352.3 1.8 copy-start.7
  363.0 2.5 copy-start
  363.9 1.8 copy-start.6
  366.1 3.7 copy-start.21
  367.2 2.6 copy-start.28
  375.2 78.8 %copy-start.23 = (f32[448]{0:T(512)S(1)}, f32[448]{0:T(512)}, u32[]{:S(2)}) copy-start(f32[448]{0:T(512)} %param.17) | copy-start | bytes 5380
  375.2 78.9 %copy-start.26 = (f32[448]{0:T(512)S(1)}, f32[448]{0:T(512)}, u32[]{:S(2)}) copy-start(f32[448]{0:T(512)} %param.23) | copy-start | bytes 5380
  375.2 78.9 %copy-start.27 = (f32[448]{0:T(512)S(1)}, f32[448]{0:T(512)}, u32[]{:S(2)}) copy-start(f32[448]{0:T(512)} %param.20) | copy-start | bytes 5380
  454.8 4.0 copy-start.5
  454.8 4.0 copy-start.10
  454.8 4.0 copy-start.11
  454.8 4.8 copy-start.12
  459.7 12.8 %copy-start.9 = (f32[2048,64]{0,1:T(8,128)S(1)}, f32[2048,64]{0,1:T(8,128)}, u32[]{:S(2)}) copy-start(f32[2048,64]{0,1:T(8,128)} %param.16) | copy-start | bytes 1572868
  459.7 12.8 %copy-start.19 = (f32[2048,64]{0,1:T(8,128)S(1)}, f32[2048,64]{0,1:T(8,128)}, u32[]{:S(2)}) copy-start(f32[2048,64]{0,1:T(8,128)} %param.22) | copy-start | bytes 1572868
  459.7 12.8 %copy-start.20 = (f32[2048,64]{0,1:T(8,128)S(1)}, f32[2048,64]{0,1:T(8,128)}, u32[]{:S(2)}) copy-start(f32[2048,64]{0,1:T(8,128)} %param.19) | copy-start | bytes 1572868
  463.5 11.5 %copy-start.15 = (bf16[512,1024]{1,0:T(8,128)(2,1)S(1)}, bf16[512,1024]{1,0:T(8,128)(2,1)}, u32[]{:S(2)}) copy-start(bf16[512,1024]{1,0:T(8,128)(2,1)} %get-tuple-element.43) | copy-start | bytes 3145732
  463.5 12.4 %copy-start.25 = (f32[1,1024]{1,0:T(1,128)S(1)}, f32[1,1024]{1,0:T(1,128)}, u32[]{:S(2)}) copy-start(f32[1,1024]{1,0:T(1,128)} %get-tuple-element.125) | copy-start | bytes 12292
  (10 other events, 14.4 us)
Sparse Core Ops, SparseCore 0:
  209.2 130.0 reduce-scatter.2
  454.9 17.5 reduce-scatter.4

commit v2 on v1

--- a/solution.py
+++ b/solution.py
@@ -494,10 +494,10 @@
                 copy(0, 0, full, "x").wait_recv()
 
     def act(descriptor):
-        if what == "tick":
+        if what == "drain":
+            descriptor.wait_send()
+        else:
             descriptor.start()
-        else:
-            descriptor.wait_send()
 
     def spread(source, upward, downward):
         @pl.when(upward)
@@ -514,17 +514,21 @@
 
     if relation == "own":
 
-        @pl.when(valid & (zs == z))
-        def _():
-            source = mine.at[
-                pl.ds(pl.multiple_of(sub * kind.height, 16), kind.height),
-                pl.ds(kind.source_column, kind.width),
-            ]
-            spread(source, z < PLANES - 1, z > 0)
-
-        @pl.when(valid & (zs != z))
-        def _():
-            spread(None, (zs < z) & (z < PLANES - 1), (zs > z) & (z > 0))
+        if what != "tick":
+
+            @pl.when(valid & (zs == z))
+            def _():
+                source = mine.at[
+                    pl.ds(pl.multiple_of(sub * kind.height, 16), kind.height),
+                    pl.ds(kind.source_column, kind.width),
+                ]
+                spread(source, z < PLANES - 1, z > 0)
+
+        if what != "launch":
+
+            @pl.when(valid & (zs != z))
+            def _():
+                spread(None, (zs < z) & (z < PLANES - 1), (zs > z) & (z > 0))
 
         return
 
@@ -537,37 +541,51 @@
         act(copy(0, 4, core_sem.at[slot], "core"))
 
 
-def forward_step(what, refs, plan, sems, at):
+def forward_step(what, refs, plan, relations, sems, sub):
     z = place()[0]
-    for kind, order, after in plan:
+    for kind, order in plan:
         for position in range(len(order[0])):
             zs = by_plane(z, [row[position] for row in order])
-            for relation in RELATIONS:
-                sub = at
-                if what == "tick":
-                    sub = at - (after + position + HOPS[relation])
+            for relation in relations:
                 forward_block(
                     what,
                     refs[kind.__name__],
                     kind,
                     zs,
                     relation,
-                    jnp.clip(sub, 0, kind.subs - 1),
+                    jnp.minimum(sub, kind.subs - 1),
                     sems,
-                    (sub >= 0) & (sub < kind.subs),
+                    sub < kind.subs,
                 )
+
+
+def launch(refs, kinds, sems):
+    z = place()[0]
+
+    def go(sub):
+        for kind in kinds:
+            forward_block(
+                "launch",
+                refs[kind.__name__],
+                kind,
+                z,
+                "own",
+                jnp.minimum(sub, kind.subs - 1),
+                sems,
+                sub < kind.subs,
+            )
+
+    repeat(max(kind.subs for kind in kinds), go)
 
 
 NEAR_LOW = ((1, 2), (1, 2), (2, 1), (2, 1))
 ONLY_ONE = ((1,),) * PLANES
 ONLY_LAST = ((3,),) * PLANES
 NEAR = ((0, 1, 2, 3), (1, 0, 2, 3), (2, 3, 1, 0), (3, 2, 1, 0))
-PLAN_LOW = ((Broad, NEAR_LOW, 0), (Narrow, ONLY_ONE, 0))
-PLAN_UP = ((Broad, ONLY_LAST, 3),)
-PLAN_DOWN = ((Down, NEAR, 6),)
+PLAN_LOW = ((Broad, NEAR_LOW), (Narrow, ONLY_ONE))
+PLAN_UP = ((Broad, ONLY_LAST),)
+PLAN_DOWN = ((Down, NEAR),)
 PLAN_ALL = PLAN_LOW + PLAN_UP + PLAN_DOWN
-EARLY_STEPS = 6
-LATE_STEPS = 12
 
 
 BF16 = jnp.bfloat16
@@ -646,10 +664,11 @@
     attn_out,
     middle,
     input_two,
-    upward,
+    slope,
     grad_branch,
     gate_grad,
     block_out,
+    grad_down,
     own_in,
     own_down,
     ada_weights,
@@ -658,7 +677,8 @@
     up_stage,
     wide,
     active,
-    out_stage,
+    flat_branch,
+    down_stage,
     send_sem,
     recv_sem,
     core_sem,
@@ -670,6 +690,7 @@
     swap_sem,
     pair_sem,
     up_sem,
+    down_sem,
 ):
     z, x, c, y = place()
     dp = (z * 2 + x) * 2 + c
@@ -758,7 +779,17 @@
             swaps[index][1].wait()
 
     trade(0)
-    repeat(2, lambda at: forward_step("tick", refs, PLAN_LOW, sems, at))
+    launch(refs, (Broad, Narrow), sems)
+
+    @pl.when((z == 0) | (z == PLANES - 1))
+    def _():
+        launch(refs, (Down,), sems)
+
+    def pass_on(plan, relations):
+        subs = max(kind.subs for kind, _ in plan)
+        repeat(subs, lambda sub: forward_step("tick", refs, plan, relations, sems, sub))
+
+    pass_on(PLAN_LOW, ("own",))
 
     def cond_arrived(at):
         there = lax.rem(dp + at + 1, DP)
@@ -810,7 +841,13 @@
 
         repeat(2 * DP, send)
 
-    forward_step("tick", refs, PLAN_LOW, sems, 2)
+    pass_on(PLAN_LOW, ("x", "y"))
+
+    @pl.when((z > 0) & (z < PLANES - 1))
+    def _():
+        launch(refs, (Down,), sems)
+
+    pass_on(PLAN_UP, ("own",))
     trade(1)
     traded(0)
 
@@ -837,11 +874,8 @@
 
     repeat(4, shape_one)
 
-    repeat(
-        EARLY_STEPS - 3,
-        lambda at: forward_step("tick", refs, PLAN_LOW + PLAN_UP, sems, at + 3),
-    )
-    repeat(SUBS, lambda at: forward_step("core", refs, PLAN_LOW, sems, at))
+    pass_on(PLAN_LOW, ("xy",))
+    repeat(SUBS, lambda at: forward_step("core", refs, PLAN_LOW, RELATIONS, sems, at))
 
     @pl.when(dp >= 7)
     def _():
@@ -882,9 +916,21 @@
     def attention(pair):
         attend_pair(pair, queries, keys, values, mixed, log_totals)
 
-        @pl.when(lax.rem(pair, 4) == 3)
+        @pl.when(pair < SUBS)
         def _():
-            forward_step("tick", refs, PLAN_UP + PLAN_DOWN, sems, EARLY_STEPS + pair // 4)
+            forward_step("tick", refs, PLAN_UP, ("x", "y"), sems, pair)
+
+        @pl.when(pair == SUBS)
+        def _():
+            forward_step("tick", refs, PLAN_DOWN, ("own",), sems, 0)
+
+        @pl.when((pair > SUBS) & (pair <= 2 * SUBS))
+        def _():
+            forward_step("tick", refs, PLAN_UP, ("xy",), sems, pair - SUBS - 1)
+
+        @pl.when(pair == 2 * SUBS + 1)
+        def _():
+            forward_step("tick", refs, PLAN_DOWN, ("x", "y"), sems, 0)
 
     repeat(PAIRS, attention)
 
@@ -903,7 +949,7 @@
         input_two[rows] = (normalize(mid) * (1.0 + vector(4)) + vector(3)).astype(BF16)
 
     repeat(4, shape_two)
-    repeat(SUBS, lambda at: forward_step("core", refs, PLAN_UP, sems, at))
+    repeat(SUBS, lambda at: forward_step("core", refs, PLAN_UP, RELATIONS, sems, at))
     whole_copies = [
         pltpu.make_async_copy(
             own_in.at[half, pl.ds(0, HALF)],
@@ -919,9 +965,27 @@
     def up_copy(at, slot):
         return pltpu.make_async_copy(
             up_stage.at[slot],
-            upward.at[:, pl.ds(pl.multiple_of(at * tile, LANES), tile)],
+            slope.at[:, pl.ds(pl.multiple_of(at * tile, LANES), tile)],
             up_sem.at[slot],
         )
+
+    def down_grad_copy(at, slot):
+        return pltpu.make_async_copy(
+            down_stage.at[slot],
+            grad_down.at[:, pl.ds(pl.multiple_of(at * tile, LANES), tile)],
+            down_sem.at[slot],
+        )
+
+    traded(1)
+
+    def shape_branch(at):
+        columns = pl.ds(pl.multiple_of(at * 256, LANES), 256)
+        gate = modulation[:, pl.ds(pl.multiple_of(5 * D + at * 256, LANES), 256)]
+        scaled = (grad_out[:, columns].astype(F32) * gate).astype(BF16)
+        grad_branch[:, columns] = scaled
+        flat_branch[pl.ds(pl.multiple_of(at * 256, 256), 256)] = scaled.T
+
+    repeat(D // 256, shape_branch)
 
     def widen(at):
         slot = lax.rem(at, 2)
@@ -929,31 +993,41 @@
         @pl.when(at >= 2)
         def _():
             up_copy(at - 2, slot).wait()
-
+            down_grad_copy(at - 2, slot).wait()
+
+        factor = math.sqrt(2.0 / math.pi)
         for side in range(2):
             start = at * tile + side * 256
             value = from_weights(input_two, own_in, 4 * D + start, 256) + bias_of(
                 own_in, 3 * D + start, 256
             )
-            up_stage[slot, :, side * 256 : (side + 1) * 256] = value
-            inner = math.sqrt(2.0 / math.pi) * (value + 0.044715 * (value * value * value))
-            wide[:, pl.ds(pl.multiple_of(start, LANES), 256)] = (
-                0.5 * value * (1.0 + jnp.tanh(inner))
+            square = value * value
+            bent = jnp.tanh(factor * value * (1.0 + 0.044715 * square))
+            half_up = 0.5 + 0.5 * bent
+            up_stage[slot, :, side * 256 : (side + 1) * 256] = half_up + 0.5 * value * (
+                1.0 - bent * bent
+            ) * (factor + 3.0 * 0.044715 * factor * square)
+            wide[:, pl.ds(pl.multiple_of(start, LANES), 256)] = (value * half_up).astype(BF16)
+        up_copy(at, slot).start()
+        for side in range(2):
+            columns = pl.ds(pl.multiple_of(at * tile + side * 256, LANES), 256)
+            down_stage[slot, :, side * 256 : (side + 1) * 256] = multiply(
+                flat_branch[...], wide[:, columns]
             ).astype(BF16)
-        up_copy(at, slot).start()
-
-        @pl.when(lax.rem(at, 2) == 1)
+        down_grad_copy(at, slot).start()
+
+        @pl.when(at == 3)
         def _():
-            forward_step("tick", refs, PLAN_DOWN, sems, EARLY_STEPS + 2 + at // 2)
+            forward_step("tick", refs, PLAN_DOWN, ("xy",), sems, 0)
 
     repeat(FF // tile, widen)
     for at in (FF // tile - 2, FF // tile - 1):
         up_copy(at, at % 2).wait()
-    forward_step("core", refs, PLAN_DOWN, sems, 0)
+        down_grad_copy(at, at % 2).wait()
+    forward_step("core", refs, PLAN_DOWN, RELATIONS, sems, 0)
     down.wait()
     down_copy = pltpu.make_async_copy(own_down, whole_down, local_sem.at[5])
     down_copy.start()
-    traded(1)
 
     def narrow_down(at):
         columns = pl.ds(pl.multiple_of(at * 256, LANES), 256)
@@ -965,26 +1039,13 @@
                 BOTH_LAST,
             )
         gate = modulation[:, pl.ds(pl.multiple_of(5 * D + at * 256, LANES), 256)]
-        out_stage[:, columns] = (middle[:, columns] + gate * value).astype(BF16)
+        block_out[:, columns] = (middle[:, columns] + gate * value).astype(BF16)
         towards = grad_out[:, columns].astype(F32)
         gate_grad[:, columns] = jnp.sum(towards * value, axis=0, keepdims=True)
-        grad_branch[:, columns] = (towards * gate).astype(BF16)
 
     repeat(D // 256, narrow_down)
-    home = pltpu.make_async_copy(out_stage, block_out, swap_sem.at[2, 0])
-    away = remote(out_stage, block_out, swap_sem.at[2, 1], swap_sem.at[2, 2], near["swap"])
-
-    @pl.when(at_home)
-    def _():
-        home.start()
-        home.wait()
-
-    @pl.when(jnp.logical_not(at_home))
-    def _():
-        away.start()
-        away.wait()
-
-    repeat(SUBS, lambda at: forward_step("drain", refs, PLAN_ALL, sems, at))
+
+    repeat(SUBS, lambda at: forward_step("drain", refs, PLAN_ALL, RELATIONS, sems, at))
     repeat(DP - 1, lambda at: cond_copy(at).wait_send())
 
     @pl.when(dp < 7)
@@ -1023,7 +1084,8 @@
         (shape((rows, FF), F32), pl.ANY),
         (shape((rows, D), BF16), pltpu.VMEM),
         (shape((1, D), F32), pltpu.VMEM),
-        (shape((rows, D), BF16), pl.ANY),
+        (shape((rows, D), BF16), pltpu.VMEM),
+        (shape((D, FF), BF16), pl.ANY),
     ]
     dma = pltpu.SemaphoreType.DMA
     return pl.pallas_call(
@@ -1041,7 +1103,8 @@
             pltpu.VMEM((2, rows, 512), F32),
             pltpu.VMEM((rows, FF), BF16),
             pltpu.VMEM((DP, D), BF16),
-            pltpu.VMEM((rows, D), BF16),
+            pltpu.VMEM((D, rows), BF16),
+            pltpu.VMEM((2, D, 512), BF16),
             dma((SLOTS, 5)),
             dma((SLOTS, 2)),
             dma((SLOTS,)),
@@ -1050,8 +1113,9 @@
             dma((DP,)),
             dma((2 * DP,)),
             dma((14,)),
-            dma((3, 3)),
+            dma((2, 3)),
             dma((2, 2)),
+            dma((2,)),
             dma((2,)),
         ],
         compiler_params=pltpu.CompilerParams(
@@ -1061,7 +1125,7 @@
     )(low_in, low_down, hidden_in, cotangent, condition, ada_bias)
 
 
-GRAD_SUBS = 4
+GRAD_SUBS = 8
 GRAD_ROWS = HALF // GRAD_SUBS
 
 
@@ -1208,6 +1272,10 @@
         pl.when(condition)(descriptor.start)
 
 
+LAGS = {"xy": 0, "x": 1, "y": 1, "own": 2}
+Z_LAG = 1
+
+
 def reduce_step(what, refs, plan, sems, at):
     z = place()[0]
     for kind, planes in plan:
@@ -1229,7 +1297,7 @@
                                 for place_z in range(PLANES)
                             ],
                         )
-                    sub = at - (2 - HOPS[relation] + depth)
+                    sub = at - (LAGS[relation] + Z_LAG * depth)
                 reduce_block(
                     what,
                     refs[name],
@@ -1260,7 +1328,7 @@
     z, x, c, y = place()
     near = neighbours()
     barrier = pltpu.get_barrier_semaphore()
-    for key in ("x", "y", "core"):
+    for key in ("x", "y", "core", "swap"):
         pl.semaphore_signal(barrier, inc=1, device_id=near[key], device_id_type=MESH)
 
     @pl.when(z < PLANES - 1)
@@ -1275,11 +1343,11 @@
 
     @pl.when(middle)
     def _():
+        pl.semaphore_wait(barrier, 6)
+
+    @pl.when(jnp.logical_not(middle))
+    def _():
         pl.semaphore_wait(barrier, 5)
-
-    @pl.when(jnp.logical_not(middle))
-    def _():
-        pl.semaphore_wait(barrier, 4)
 
 
 REDUCE_HIGH = ((BroadGrad, (3,)),)
@@ -1331,22 +1399,39 @@
     grad_mixed,
     log_totals,
     grads,
+    block_out,
     grad_query,
     grad_key,
     grad_value,
     owned,
+    block_swapped,
     key_all,
     value_all,
     key_mate,
     value_mate,
     mate_sem,
+    swap_sem,
     *scratch,
 ):
     dp = lax.axis_index("dp")
+    at_home = lax.rem(dp, 2) == lax.axis_index("seq")
     near = neighbours()
     refs = {"BroadGrad": (grads, 4 * D, owned, scratch[:7])}
     sems = {"BroadGrad": scratch[7:9]}
     greet_near()
+    away = pltpu.make_async_remote_copy(
+        src_ref=block_out,
+        dst_ref=block_swapped,
+        send_sem=swap_sem.at[0],
+        recv_sem=swap_sem.at[1],
+        device_id=near["swap"],
+        device_id_type=MESH,
+    )
+
+    @pl.when(jnp.logical_not(at_home))
+    def _():
+        away.start()
+
     repeat(GRAD_SUBS, lambda at: reduce_step("across", refs, REDUCE_HIGH, sems, at))
 
     @pl.when(dp < 12)
@@ -1396,19 +1481,25 @@
     )
     repeat(GRAD_SUBS, lambda at: reduce_step("drain", refs, REDUCE_HIGH, sems, at))
 
-
-def run_backward(queries, keys, values, mixed, grad_mixed, log_totals, grads):
+    @pl.when(jnp.logical_not(at_home))
+    def _():
+        away.wait()
+
+
+def run_backward(queries, keys, values, mixed, grad_mixed, log_totals, grads, block_out):
     shape = jax.ShapeDtypeStruct
     rows = TOKENS_HERE
     vmem = pl.BlockSpec(memory_space=pltpu.VMEM)
+    hbm = pl.BlockSpec(memory_space=pl.ANY)
     return pl.pallas_call(
         backward_kernel,
-        out_shape=[shape((rows, D), BF16)] * 3 + [shape((HALF, WIDE), F32)],
-        in_specs=[vmem] * 7,
-        out_specs=[vmem] * 4,
+        out_shape=[shape((rows, D), BF16)] * 3
+        + [shape((HALF, WIDE), F32), shape((rows, D), BF16)],
+        in_specs=[vmem] * 7 + [hbm],
+        out_specs=[vmem] * 4 + [hbm],
         scratch_shapes=[pltpu.VMEM((2 * rows, D), BF16)] * 2
         + [pltpu.VMEM((rows, D), BF16)] * 2
-        + [pltpu.SemaphoreType.DMA((PAIRS, 4))]
+        + [pltpu.SemaphoreType.DMA((PAIRS, 4)), pltpu.SemaphoreType.DMA((2,))]
         + landing(BroadGrad, 1)
         + landing_signals(BroadGrad, 1),
         compiler_params=pltpu.CompilerParams(
@@ -1418,7 +1509,7 @@
             flops=5 * 2 * 512 * 1024 * 1024 * 2, bytes_accessed=60 * 2**20, transcendentals=2**23
         ),
         name="backward",
-    )(queries, keys, values, mixed, grad_mixed, log_totals, grads)
+    )(queries, keys, values, mixed, grad_mixed, log_totals, grads, block_out)
 
 
 VECTOR = 17 * WIDE
@@ -1434,10 +1525,12 @@
     sums,
     input_grad,
     owned_high,
+    down_sum,
     owned,
     cond_grad,
     bias_parts,
     ada_bias_grad,
+    owned_down,
     input_swapped,
     grads,
     ada_weights,
@@ -1446,8 +1539,10 @@
     ada_in,
     cond_piece,
     cond_in,
+    down_mate,
     local_sem,
     mate_sem,
+    down_sem,
     piece_send,
     ada_recv,
     bias_recv,
@@ -1490,6 +1585,14 @@
     greet_all()
     mate = remote(sums, sum_mate, mate_sem.at[0], mate_sem.at[1], near["core"])
     mate.start()
+    down_away = remote(
+        down_sum.at[:, pl.ds(pl.multiple_of((1 - y) * FF_PART, LANES), FF_PART)],
+        down_mate,
+        down_sem.at[0],
+        down_sem.at[1],
+        near["y"],
+    )
+    down_away.start()
     away = remote(input_grad, input_swapped, swap_sem.at[0], swap_sem.at[1], near["swap"])
 
     for load in loads[:3]:
@@ -1633,6 +1736,10 @@
     def _():
         away.wait()
 
+    down_away.wait()
+    owned_down[...] = down_sum[
+        :, pl.ds(pl.multiple_of(y * FF_PART, LANES), FF_PART)
+    ].astype(F32) + down_mate[...].astype(F32)
     each_piece(lambda copy: copy.wait_send(), False)
 
     @pl.when(dp < 7)
@@ -1643,7 +1750,16 @@
 
 
 def run_finish(
-    grad_qkv, grad_out_proj, grad_up, low_in, active_rows, condition, sums, input_grad, owned_high
+    grad_qkv,
+    grad_out_proj,
+    grad_up,
+    low_in,
+    active_rows,
+    condition,
+    sums,
+    input_grad,
+    owned_high,
+    down_sum,
 ):
     shape = jax.ShapeDtypeStruct
     dma = pltpu.SemaphoreType.DMA
@@ -1656,10 +1772,11 @@
             shape((1, D), F32),
             shape((DP, 1, WIDE), F32),
             shape((1, WIDE), F32),
+            shape((64, FF_PART), F32),
             shape((TOKENS_HERE, D), BF16),
         ],
-        in_specs=[hbm] * 4 + [vmem] * 3 + [hbm, vmem],
-        out_specs=[vmem] * 4 + [hbm],
+        in_specs=[hbm] * 4 + [vmem] * 3 + [hbm, vmem, vmem],
+        out_specs=[vmem] * 5 + [hbm],
         scratch_shapes=[
             pltpu.VMEM((D, 4 * D + HIGH_FIRST), BF16),
             pltpu.VMEM((HALF, WIDE), BF16),
@@ -1668,7 +1785,9 @@
             pltpu.VMEM((DP, 1, WIDE), F32),
             pltpu.VMEM((DP, 1, HALF), F32),
             pltpu.VMEM((14, 1, HALF), F32),
+            pltpu.VMEM((64, FF_PART), BF16),
             dma((4,)),
+            dma((2,)),
             dma((2,)),
             dma((17,)),
             dma((DP,)),
@@ -1685,7 +1804,18 @@
             collective_id=2, has_side_effects=True, vmem_limit_bytes=60 * 2**20
         ),
         name="finish",
-    )(grad_qkv, grad_out_proj, grad_up, low_in, active_rows, condition, sums, input_grad, owned_high)
+    )(
+        grad_qkv,
+        grad_out_proj,
+        grad_up,
+        low_in,
+        active_rows,
+        condition,
+        sums,
+        input_grad,
+        owned_high,
+        down_sum,
+    )
 
 
 def local(
@@ -1725,10 +1855,11 @@
         attn_out,
         middle,
         input_two,
-        upward,
+        slope,
         grad_branch,
         gate_two_grad,
         block_out,
+        grad_down,
     ) = run_forward(
         low_in,
         weights_down.astype(BF16).T,
@@ -1755,10 +1886,9 @@
     def down_rows(total):
         return jnp.sum(total.astype(F32), axis=0, keepdims=True)
 
-    activated, gelu_pull = jax.vjp(lambda inner: jax.nn.gelu(inner, approximate=True), upward)
-    grad_down = outer(activated.astype(BF16), grad_branch)
+    down_sum = lax.psum_scatter(grad_down, "dp", scatter_dimension=0, tiled=True)
     grad_act = jnp.dot(grad_branch, whole_down, preferred_element_type=F32)
-    grad_upward = gelu_pull(grad_act)[0].astype(BF16)
+    grad_upward = (grad_act * slope).astype(BF16)
     grad_up = outer(input_two, grad_upward).astype(BF16)
     grad_input_two = back_through(grad_upward, 4 * D, FF)
     normed_two, norm_pull_two = jax.vjp(layer_norm, middle)
@@ -1769,12 +1899,11 @@
     gate_one_grad = down_rows(grad_middle * attn_out)
     grad_out_proj = outer(mixed, grad_attn).astype(BF16)
     grad_mixed = back_through(grad_attn, 3 * D, D).astype(BF16)
-    down_sum = lax.psum_scatter(
-        grad_down.astype(BF16), "dp", scatter_dimension=1, tiled=True
-    )
-    grad_query, grad_key, grad_value, owned_high = run_backward(
-        queries, keys, values, mixed, grad_mixed, log_totals, grad_up
-    )
+    at_home = lax.rem(dp, 2) == y
+    grad_query, grad_key, grad_value, owned_high, block_swapped = run_backward(
+        queries, keys, values, mixed, grad_mixed, log_totals, grad_up, block_out
+    )
+    block_out = jnp.where(at_home, block_out, block_swapped)
     grad_qkv = jnp.concatenate([grad_query, grad_key, grad_value], axis=-1)
     grad_proj_qkv = outer(input_one, grad_qkv).astype(BF16)
     grad_input_one = back_through(grad_qkv, 0, 3 * D)
@@ -1802,7 +1931,7 @@
     active_rows = lax.dynamic_slice_in_dim(
         jax.nn.silu(cond_all[:, 0]).astype(BF16), y * HALF, HALF, 1
     )
-    owned_in, cond_grad, bias_parts, ada_bias_grad, input_swapped = run_finish(
+    owned_in, cond_grad, bias_parts, ada_bias_grad, owned_down, input_swapped = run_finish(
         grad_proj_qkv,
         grad_out_proj,
         grad_up,
@@ -1812,10 +1941,10 @@
         sums,
         input_grad.astype(BF16),
         owned_high,
-    )
-    at_home = lax.rem(dp, 2) == y
+        down_sum,
+    )
+    owned_down = owned_down.T
     input_grad = jnp.where(at_home, input_grad, input_swapped.astype(F32))
-    owned_down = lax.psum_scatter(down_sum, "seq", scatter_dimension=0, tiled=True).astype(F32)
     owned_bias = jnp.sum(bias_parts[:, 0], axis=0) + ada_bias_grad[0]
     owned_bias = lax.dynamic_slice_in_dim(owned_bias, y * side, side, 0)
     moments_in, squares_in, master_in = adamw_step(

time: 493 us -> 449 us (0.911)
  Pallas kernels: 365 us -> 347 us
  matrix products: 59.5 us -> 43.1 us
  waiting for transfers between devices: 9.07 us -> 0.04 us
    pallas_call x1, Pallas kernels: 185 us -> 164 us  [run_forward(): pl.pallas_call(forward_kernel, out_shape=[one for one, _ in outs], in_spe...]
    dot_general x4 -> x3, matrix products: 24.3 us -> 15.1 us  [outer(): return lax.dot_general(left, right, BOTH_FIRST, preferred_element_type=F32)]
    reduce_scatter x2 -> x1, waiting for transfers between devices: 9.04 us -> 0.02 us  [local(): lax.psum_scatter(grad_down, 'dp', scatter_dimension=0, tiled=True)]
    pallas_call x1, Pallas kernels: 77.2 us -> 83.7 us  [run_finish(): pl.pallas_call(finish_kernel, out_shape=[shape((HALF, WIDE), F32), shape(...]
    dot_general x1, matrix products: 14.9 us -> 9.41 us  [local(): grad_act = jnp.dot(grad_branch, whole_down, preferred_element_type=F32)]
  transfers between devices with their start and end apart: 2 -> 1, of which waited for: 1 -> 0; matrix products, arithmetic and copies ran while one was open for 14% -> 12% of each run, Pallas kernels for 37% -> 23%
where the time goes in v2:
time: 449 us; the launch traced here: 442 us
  Pallas kernels  347 us (77%)
  matrix products  43.1 us (10%)
  other arithmetic  28.2 us (6%)
  between operations  14.9 us (3%)
  local copies, waits for them, and re-layouts  8.03 us (2%)
    pallas_call x1, Pallas kernels, run_forward(): pl.pallas_call(forward_kernel, out_shape=[one for one, _ in outs], in_spe...  164 us
    pallas_call x1, Pallas kernels, run_backward(): pl.pallas_call(backward_kernel, out_shape=[shape((rows, D), BF16)] * 3 +...  99.8 us
    pallas_call x1, Pallas kernels, run_finish(): pl.pallas_call(finish_kernel, out_shape=[shape((HALF, WIDE), F32), shape(...  83.7 us
    dot_general x3, matrix products, back_through(): lax.dot_general(gradients, whole_in[:, start:start + width], BOTH_LAST, p...  18.6 us
    dot_general x3, matrix products, outer(): return lax.dot_general(left, right, BOTH_FIRST, preferred_element_type=F32)  15.1 us
    dot_general x1, matrix products, local(): grad_act = jnp.dot(grad_branch, whole_down, preferred_element_type=F32)  9.41 us
  transfers between devices with their start and end apart: 1, of which 0 were waited for; matrix products, arithmetic and copies ran while one was open for 12% of the time, Pallas kernels for 23%

profile of v2, /device:TPU:19, one launch (start us, length us, event | category | flops | bytes accessed | tf_op | source)
XLA Modules:
  0.0 441.7 jit_solution(12387911685954916462)
XLA Ops:
  7.9 1.3 convert_element_type.77.condition
  9.9 1.8 convert_bitcast_fusion.low_down
  11.7 1.6 convert_element_type.74
  13.3 1.0 pad_maximum_fusion.low_in
  14.3 164.1 %forward.1 = (bf16[1024,8192]{1,0:T(8,128)(2,1)}, bf16[1024,4096]{1,0:T(8,128)(2,1)}, bf16[512,1024]{1,0:T(8,128)(2,1)}, bf16[512,1024]{1,0:T(8,128)(2,1)}, f32[...) custom-call(bf16[528,896]{1,0:T(8,128)(2,1)} %pad_maximum_fusion.low, ...), custom_call_target="tpu_custom_call" | custom-call | tf_op jit(solution)/shard_map/forward/pallas_call | solution.py:1091
  178.4 1.5 copy-done
  181.2 9.4 %convert_reduce_fusion = (f32[4096]{0:T(1024)S(1)}, bf16[512,4096]{1,0:T(8,128)(2,1)S(1)}) fusion(f32[512,4096]{1,0:T(8,128)} %get-tuple-element.54, bf16[512,1024]{1,0:T(8,128)(2,1)S(1)} %copy-done.10, bf16[1024,4096]{1,0:T(8,128)(2,1)} %get-tuple-element.53), kind=kOutput, calls=%fused_computation | convolution fusion | flops 4303351808 | bytes 22036480 | tf_op jit(solution)/shard_map/dot_general | solution.py:1890
  191.3 8.1 %multiply_reduce_fusion = (f32[1024]{0:T(1024)S(1)}, f32[512]{0:T(512)S(1)}, f32[1024]{0:T(1024)S(1)}, f32[512,1024]{1,0:T(8,128)S(1)}) fusion(f32[512,1024]{1,0:T(8,128)S(1)} %copy-done, f32[512]{0:T(512)S(1)} %fusion.21, f32[512]{0:T(512)S(1)} %broadcast_multiply_fusion.1, f32[1024]{0:T(1024)S(1)} %bitcast.52, ...), kind=kOutput, calls=%fused_computation.27 | convolution fusion | flops 4299159040 | bytes 16795648 | tf_op jit(solution)/shard_map/dot_general | solution.py:1876
  201.2 4.5 %fusion.15.grad_mixed = bf16[512,1024]{1,0:T(8,128)(2,1)} fusion(bf16[512,1024]{1,0:T(8,128)(2,1)S(1)} %get-tuple-element.98, bf16[1024,8192]{1,0:T(8,128)(2,1)} %get-tuple-element.55), kind=kOutput, calls=%fused_computation.39 | convolution fusion | flops 1074266112 | bytes 4194304 | tf_op jit(solution)/shard_map/dot_general | solution.py:1876
  205.6 6.8 %convolution_convert_fusion.grads.grad_up = bf16[1024,4096]{1,0:T(8,128)(2,1)} fusion(bf16[512,1024]{1,0:T(8,128)(2,1)S(1)} %copy-done.28, bf16[512,4096]{1,0:T(8,128)(2,1)S(1)} %get-tuple-element.109), kind=kOutput, calls=%fused_computation.4 | convolution fusion | flops 4299161600 | bytes 13631488 | tf_op jit(solution)/shard_map/dot_general | solution.py:1884
  212.4 99.8 %backward.1 = (bf16[512,1024]{1,0:T(8,128)(2,1)}, bf16[512,1024]{1,0:T(8,128)(2,1)}, bf16[512,1024]{1,0:T(8,128)(2,1)}, f32[512,896]{1,0:T(8,128)}, bf16[512,1024]{1,0:T(8,128)(2,1)}) custom-call(bf16[512,1024]{1,0:T(8,128)(2,1)} %get-tuple-element.47.queries, bf16[1024,1024]{1,0:T(8,128)(2,1)} %get-tuple-element.48.keys, ...), custom_call_target="tpu_custom_call" | custom-call | flops 10737418240 | bytes 62914560 | tf_op jit(solution)/shard_map/backward/pallas_call | solution.py:1494
  312.2 1.4 constant_dynamic-update-slice_fusion.2
  314.1 0.9 copy-done.3
  316.1 6.1 %fusion.9 = (f32[512]{0:T(512)S(1)}, f32[1024]{0:T(1024)S(1)}, f32[1024]{0:T(1024)S(1)}, f32[512,1024]{1,0:T(8,128)S(1)}) fusion(bf16[512,1024]{1,0:T(8,128)(2,1)S(1)} %copy-done.3, f32[512]{0:T(512)S(1)} %broadcast_multiply_fusion, f32[1024]{0:T(1024)S(1)} %bitcast.49, f32[512]{0:T(512)S(1)} %fusion.22, ...), kind=kOutput, calls=%fused_computation.19 | convolution fusion | flops 3225941504 | bytes 12601344 | tf_op jit(solution)/shard_map/dot_general | solution.py:1876
  322.2 0.7 fusion.29
  323.0 0.8 copy-done.8
  323.8 1.7 fusion.19
  327.1 1.1 select_bitcast_fusion.1
  328.2 2.6 convolution_convert_fusion.2.grad_out_proj
  330.8 5.7 %convolution_convert_fusion.1.grad_qkv = bf16[1024,3072]{1,0:T(8,128)(2,1)} fusion(bf16[512,1024]{1,0:T(8,128)(2,1)S(1)} %copy-done.26, bf16[512,3072]{1,0:T(8,128)(2,1)S(1)} %constant_dynamic-update-slice_fusion), kind=kOutput, calls=%fused_computation.7 | convolution fusion | flops 3224371200 | bytes 10485760 | tf_op jit(solution)/shard_map/dot_general | solution.py:1884
  336.5 83.7 %finish.1 = (f32[512,896]{1,0:T(8,128)}, f32[1,1024]{1,0:T(1,128)}, f32[16,1,896]{2,1,0:T(1,128)}, f32[1,896]{1,0:T(1,128)}, f32[64,2048]{1,0:T(8,128)}, /*index=5*/bf16[512,1024]{1,0:T(8,128)(2,1)}) custom-call(bf16[1024,3072]{1,0:T(8,128)(2,1)} %convolution_convert_fusion.1.grad_qkv, bf16[1024,1024]{1,0:T(8,128)(2,1)} %convolution_convert_fusion.2.grad_out_proj, ...), custom_call_target="tpu_custom_call" | custom-call | tf_op jit(solution)/shard_map/finish/pallas_call | solution.py:1768
  420.2 3.8 select_bitcast_fusion
  424.1 3.2 fusion.25
  427.3 5.8 %fusion.27 = (bf16[512,896]{1,0:T(8,128)(2,1)}, f32[512,896]{1,0:T(8,128)}, f32[512,896]{1,0:T(8,128)}, f32[512,896]{1,0:T(8,128)}) fusion(f32[512,896]{1,0:T(8,128)S(1)} %copy-done.5, f32[512,896]{1,0:T(8,128)} %get-tuple-element.73, f32[512,896]{1,0:T(8,128)S(1)} %copy-done.9, f32[512,896]{1,0:T(8,128)} %param.18), kind=kLoop, calls=%fused_computation.86 | loop fusion | flops 6881280 | bytes 13762560 | tf_op jit(solution)/shard_map/convert_element_type | solution.py:1972
  (100 shorter events, 9.6 us)
Async XLA Ops:
  7.2 329.3 %reduce-scatter.2.cloned.1.call-start = ((), (), s32[]{:S(2)}) async-start(), calls=%async_computation.1 | async-start | bytes 8912896 | tf_op jit(solution)/shard_map/reduce_scatter | solution.py:1889
  178.3 1.6 copy-start
  191.3 8.1 %copy-start.1 = (f32[512,1024]{1,0:T(8,128)S(1)}, f32[512,1024]{1,0:T(8,128)}, u32[]{:S(2)}) copy-start(f32[512,1024]{1,0:T(8,128)} %get-tuple-element.57) | copy-start | bytes 6291460
  201.2 4.5 %copy-start.15 = (bf16[512,1024]{1,0:T(8,128)(2,1)}, bf16[512,1024]{1,0:T(8,128)(2,1)S(1)}, u32[]{:S(2)}) copy-start(bf16[512,1024]{1,0:T(8,128)(2,1)S(1)} %get-tuple-element.98) | copy-start | bytes 3145732
  201.2 4.5 %copy-start.28 = (bf16[512,1024]{1,0:T(8,128)(2,1)S(1)}, bf16[512,1024]{1,0:T(8,128)(2,1)}, u32[]{:S(2)}) copy-start(bf16[512,1024]{1,0:T(8,128)(2,1)} %get-tuple-element.59) | copy-start | bytes 3145732
  312.2 1.8 copy-start.7
  313.7 1.6 copy-start.11
  322.2 1.6 copy-start.8
  323.0 2.5 copy-start.2
  323.8 1.7 copy-start.21
  323.8 1.8 copy-start.6
  325.5 1.6 copy-start.13
  325.9 2.2 copy-start.16
  325.9 2.2 copy-start.27
  326.0 4.8 %copy-start.17 = (f32[1,15232]{1,0:T(1,128)}, f32[1,15232]{1,0:T(1,128)S(1)}, u32[]{:S(2)}) copy-start(f32[1,15232]{1,0:T(1,128)S(1)} %constant_dynamic-update-slice_fusion.3.sums) | copy-start | bytes 182788
  328.2 2.6 copy-start.26
  420.2 3.8 copy-start.19
  420.2 3.9 copy-start.23
  424.0 3.3 copy-start.5
  424.1 3.2 copy-start.9
  427.3 5.8 %copy-start.20 = (f32[448]{0:T(512)S(1)}, f32[448]{0:T(512)}, u32[]{:S(2)}) copy-start(f32[448]{0:T(512)} %param.17) | copy-start | bytes 5380
  427.3 5.8 %copy-start.24 = (f32[448]{0:T(512)S(1)}, f32[448]{0:T(512)}, u32[]{:S(2)}) copy-start(f32[448]{0:T(512)} %param.23) | copy-start | bytes 5380
  427.3 5.8 %copy-start.25 = (f32[448]{0:T(512)S(1)}, f32[448]{0:T(512)}, u32[]{:S(2)}) copy-start(f32[448]{0:T(512)} %param.20) | copy-start | bytes 5380
  427.3 6.5 %copy-start.22 = (f32[1,1024]{1,0:T(1,128)S(1)}, f32[1,1024]{1,0:T(1,128)}, u32[]{:S(2)}) copy-start(f32[1,1024]{1,0:T(1,128)} %get-tuple-element.131) | copy-start | bytes 12292
  (6 other events, 7.5 us)
Sparse Core Ops, SparseCore 0:
  178.5 127.8 reduce-scatter.1

commit v3 on v2

--- a/solution.py
+++ b/solution.py
@@ -399,7 +399,7 @@
 
 
 class Broad:
-    height, width, subs, split = SUB_ROWS, WIDE, SUBS, 96
+    height, width, subs, split = SUB_ROWS, WIDE, SUBS, 64
     first, source_column = 0, 0
 
     @staticmethod
@@ -651,22 +651,22 @@
     ada_bias,
     whole_in,
     whole_down,
-    hidden,
-    grad_out,
+    hidden_out,
+    grad_out_out,
     cond_all,
     modulation,
-    input_one,
-    queries,
-    keys,
-    values,
-    mixed,
+    input_one_out,
+    queries_out,
+    keys_out,
+    values_out,
+    mixed_out,
     log_totals,
-    attn_out,
-    middle,
-    input_two,
+    attn_out_out,
+    middle_out,
+    input_two_out,
     slope,
-    grad_branch,
-    gate_grad,
+    grad_branch_out,
+    row_grads,
     block_out,
     grad_down,
     own_in,
@@ -691,6 +691,18 @@
     pair_sem,
     up_sem,
     down_sem,
+    hidden,
+    grad_out,
+    input_one,
+    queries,
+    keys,
+    values,
+    mixed,
+    attn_out,
+    middle,
+    input_two,
+    grad_branch,
+    keep_sem,
 ):
     z, x, c, y = place()
     dp = (z * 2 + x) * 2 + c
@@ -708,6 +720,29 @@
             device_id=device,
             device_id_type=MESH,
         )
+
+    kept = {
+        name: pltpu.make_async_copy(source, target, keep_sem.at[index])
+        for index, (name, source, target) in enumerate(
+            (
+                ("hidden", hidden, hidden_out),
+                ("grad_out", grad_out, grad_out_out),
+                ("input_one", input_one, input_one_out),
+                ("queries", queries, queries_out),
+                ("keys", keys, keys_out),
+                ("values", values, values_out),
+                ("mixed", mixed, mixed_out),
+                ("attn_out", attn_out, attn_out_out),
+                ("middle", middle, middle_out),
+                ("input_two", input_two, input_two_out),
+                ("grad_branch", grad_branch, grad_branch_out),
+            )
+        )
+    }
+
+    def keep(*which):
+        for name in which:
+            kept[name].start()
 
     broad = pltpu.make_async_copy(
         low_in,
@@ -873,6 +908,7 @@
         input_one[rows] = (normed * (1.0 + vector(1)) + vector(0)).astype(BF16)
 
     repeat(4, shape_one)
+    keep("hidden", "input_one")
 
     pass_on(PLAN_LOW, ("xy",))
     repeat(SUBS, lambda at: forward_step("core", refs, PLAN_LOW, RELATIONS, sems, at))
@@ -912,6 +948,7 @@
     repeat(D // 256, project_queries)
     for mate in mates:
         mate.wait()
+    keep("queries", "keys", "values")
 
     def attention(pair):
         attend_pair(pair, queries, keys, values, mixed, log_totals)
@@ -933,6 +970,7 @@
             forward_step("tick", refs, PLAN_DOWN, ("x", "y"), sems, 0)
 
     repeat(PAIRS, attention)
+    keep("mixed")
 
     def project_out(at):
         columns = pl.ds(pl.multiple_of(at * 256, LANES), 256)
@@ -949,6 +987,7 @@
         input_two[rows] = (normalize(mid) * (1.0 + vector(4)) + vector(3)).astype(BF16)
 
     repeat(4, shape_two)
+    keep("attn_out", "middle", "input_two")
     repeat(SUBS, lambda at: forward_step("core", refs, PLAN_UP, RELATIONS, sems, at))
     whole_copies = [
         pltpu.make_async_copy(
@@ -984,8 +1023,10 @@
         scaled = (grad_out[:, columns].astype(F32) * gate).astype(BF16)
         grad_branch[:, columns] = scaled
         flat_branch[pl.ds(pl.multiple_of(at * 256, 256), 256)] = scaled.T
+        row_grads[1:2, columns] = jnp.sum(scaled.astype(F32), axis=0, keepdims=True)
 
     repeat(D // 256, shape_branch)
+    keep("grad_out", "grad_branch")
 
     def widen(at):
         slot = lax.rem(at, 2)
@@ -1041,7 +1082,7 @@
         gate = modulation[:, pl.ds(pl.multiple_of(5 * D + at * 256, LANES), 256)]
         block_out[:, columns] = (middle[:, columns] + gate * value).astype(BF16)
         towards = grad_out[:, columns].astype(F32)
-        gate_grad[:, columns] = jnp.sum(towards * value, axis=0, keepdims=True)
+        row_grads[0:1, columns] = jnp.sum(towards * value, axis=0, keepdims=True)
 
     repeat(D // 256, narrow_down)
 
@@ -1060,33 +1101,38 @@
     for whole_copy in whole_copies:
         whole_copy.wait()
     down_copy.wait()
+    for one in kept.values():
+        one.wait()
 
 
 def run_forward(low_in, low_down, hidden_in, cotangent, condition, ada_bias):
     shape = jax.ShapeDtypeStruct
     rows = TOKENS_HERE
+    wide, flat = shape((rows, D), BF16), shape((rows, D), F32)
+    both = shape((2 * rows, D), BF16)
     outs = [
         (shape((D, KEPT), BF16), pl.ANY),
         (shape((D, FF), BF16), pl.ANY),
-        (shape((rows, D), BF16), pltpu.VMEM),
-        (shape((rows, D), BF16), pltpu.VMEM),
+        (wide, pl.ANY),
+        (wide, pl.ANY),
         (shape((DP, 1, D), F32), pltpu.VMEM),
         (shape((1, 7 * WIDE), F32), pltpu.VMEM),
-        (shape((rows, D), BF16), pltpu.VMEM),
-        (shape((rows, D), BF16), pltpu.VMEM),
-        (shape((2 * rows, D), BF16), pltpu.VMEM),
-        (shape((2 * rows, D), BF16), pltpu.VMEM),
-        (shape((rows, D), BF16), pltpu.VMEM),
+        (wide, pl.ANY),
+        (wide, pl.ANY),
+        (both, pl.ANY),
+        (both, pl.ANY),
+        (wide, pl.ANY),
         (shape((HEADS, 1, rows), F32), pltpu.VMEM),
-        (shape((rows, D), F32), pltpu.VMEM),
-        (shape((rows, D), F32), pltpu.VMEM),
-        (shape((rows, D), BF16), pltpu.VMEM),
+        (flat, pl.ANY),
+        (flat, pl.ANY),
+        (wide, pl.ANY),
         (shape((rows, FF), F32), pl.ANY),
-        (shape((rows, D), BF16), pltpu.VMEM),
-        (shape((1, D), F32), pltpu.VMEM),
-        (shape((rows, D), BF16), pltpu.VMEM),
+        (wide, pl.ANY),
+        (shape((8, D), F32), pltpu.VMEM),
+        (wide, pltpu.VMEM),
         (shape((D, FF), BF16), pl.ANY),
     ]
+    kept = (wide, wide, wide, wide, both, both, wide, flat, flat, wide, wide)
     dma = pltpu.SemaphoreType.DMA
     return pl.pallas_call(
         forward_kernel,
@@ -1117,7 +1163,9 @@
             dma((2, 2)),
             dma((2,)),
             dma((2,)),
-        ],
+        ]
+        + [pltpu.VMEM(one.shape, one.dtype) for one in kept]
+        + [dma((len(kept),))],
         compiler_params=pltpu.CompilerParams(
             collective_id=0, has_side_effects=True, vmem_limit_bytes=62 * 2**20
         ),
@@ -1131,6 +1179,7 @@
 
 class BroadGrad:
     height, width, subs, source_column = GRAD_ROWS, WIDE, GRAD_SUBS, 0
+    split = GRAD_ROWS // 2
 
     @staticmethod
     def holds(zs, xs, cs):
@@ -1145,8 +1194,13 @@
         )
 
 
+class HighGrad(BroadGrad):
+    split = 48
+
+
 class NarrowGrad:
     height, width, subs, source_column = HALF, 128, 1, WIDE - 128
+    split = HALF // 2
 
     @staticmethod
     def holds(zs, xs, cs):
@@ -1169,7 +1223,7 @@
     count = planes * kind.subs
     kin = RELATIONS.index(relation)
     slot = kin * count + flat
-    rows, half_rows = kind.height, kind.height // 2
+    rows, half_rows = kind.height, kind.split
 
     def remote(source, target, index, arrival, key):
         return pltpu.make_async_remote_copy(
@@ -1196,7 +1250,7 @@
         pl.when(other)(across.wait_send)
     valid = valid & kind.holds(zs, xs, c)
     part_a = from_core.at[slot, pl.ds(0, half_rows)]
-    part_b = from_core.at[slot, pl.ds(half_rows, half_rows)]
+    part_b = from_core.at[slot, pl.ds(half_rows, rows - half_rows)]
     if relation == "xy":
         sends = [
             (valid, remote(part_a, half_a.at[flat], 0, 4, "y")),
@@ -1224,14 +1278,14 @@
             from_core[slot] = value.astype(BF16)
         elif relation == "x":
             remote(half_a.at[flat], half_a.at[flat], 0, 4, "y").wait_recv()
-            from_core[slot, pl.ds(half_rows, half_rows)] = value[half_rows:].astype(BF16)
+            from_core[slot, pl.ds(half_rows, rows - half_rows)] = value[half_rows:].astype(BF16)
             from_core[slot, pl.ds(0, half_rows)] = (
                 value[:half_rows] + half_a[flat].astype(F32)
             ).astype(BF16)
         elif relation == "y":
             remote(half_b.at[flat], half_b.at[flat], 1, 5, "x").wait_recv()
             from_core[slot, pl.ds(0, half_rows)] = value[:half_rows].astype(BF16)
-            from_core[slot, pl.ds(half_rows, half_rows)] = (
+            from_core[slot, pl.ds(half_rows, rows - half_rows)] = (
                 value[half_rows:] + half_b[flat].astype(F32)
             ).astype(BF16)
         else:
@@ -1315,8 +1369,10 @@
 def landing(kind, planes):
     count = planes * kind.subs
     full = pltpu.VMEM((count, kind.height, kind.width), BF16)
-    half = pltpu.VMEM((count, kind.height // 2, kind.width), BF16)
-    return [pltpu.VMEM((4 * count, kind.height, kind.width), BF16)] + [full] * 4 + [half] * 2
+    half_a = pltpu.VMEM((count, kind.split, kind.width), BF16)
+    half_b = pltpu.VMEM((count, kind.height - kind.split, kind.width), BF16)
+    sums = pltpu.VMEM((4 * count, kind.height, kind.width), BF16)
+    return [sums] + [full] * 4 + [half_a, half_b]
 
 
 def landing_signals(kind, planes):
@@ -1328,7 +1384,7 @@
     z, x, c, y = place()
     near = neighbours()
     barrier = pltpu.get_barrier_semaphore()
-    for key in ("x", "y", "core", "swap"):
+    for key in ("x", "y", "core"):
         pl.semaphore_signal(barrier, inc=1, device_id=near[key], device_id_type=MESH)
 
     @pl.when(z < PLANES - 1)
@@ -1343,17 +1399,17 @@
 
     @pl.when(middle)
     def _():
-        pl.semaphore_wait(barrier, 6)
+        pl.semaphore_wait(barrier, 5)
 
     @pl.when(jnp.logical_not(middle))
     def _():
-        pl.semaphore_wait(barrier, 5)
-
-
-REDUCE_HIGH = ((BroadGrad, (3,)),)
+        pl.semaphore_wait(barrier, 4)
+
+
+REDUCE_HIGH = ((HighGrad, (3,)),)
 REDUCE_LOW = ((BroadGrad, (1, 2)), (NarrowGrad, (1,)))
 HIGH_STEPS = GRAD_SUBS + 5
-LOW_STEPS = GRAD_SUBS + 5
+LOW_STEPS = GRAD_SUBS + 4
 HIGH_FIRST = FF // 8
 
 
@@ -1392,6 +1448,25 @@
 
 
 def backward_kernel(
+    queries_in,
+    keys_in,
+    values_in,
+    mixed_in,
+    grad_mixed_in,
+    log_totals_in,
+    grads_in,
+    input_one_in,
+    hidden_in,
+    grad_middle_in,
+    grad_attn_in,
+    scale_one,
+    early_sums,
+    whole_in,
+    owned,
+    input_grad,
+    input_low,
+    sums,
+    grad_low,
     queries,
     keys,
     values,
@@ -1399,44 +1474,89 @@
     grad_mixed,
     log_totals,
     grads,
-    block_out,
+    input_one,
+    hidden,
+    grad_middle,
+    grad_attn,
+    load_sem,
     grad_query,
     grad_key,
     grad_value,
-    owned,
-    block_swapped,
+    row_sums,
     key_all,
     value_all,
     key_mate,
     value_mate,
+    flat_one,
+    weight_stage,
+    grad_stage,
+    grad_one,
     mate_sem,
-    swap_sem,
+    weight_sem,
+    grad_sem,
     *scratch,
 ):
     dp = lax.axis_index("dp")
-    at_home = lax.rem(dp, 2) == lax.axis_index("seq")
     near = neighbours()
-    refs = {"BroadGrad": (grads, 4 * D, owned, scratch[:7])}
-    sems = {"BroadGrad": scratch[7:9]}
+    refs = {"HighGrad": (grads, 4 * D, owned, scratch[:7])}
+    sems = {"HighGrad": scratch[7:9]}
+    tile = 512
+    tiles = 3 * D // tile
+    loads = [
+        pltpu.make_async_copy(source, target, load_sem.at[index])
+        for index, (source, target) in enumerate(
+            (
+                (grads_in, grads),
+                (input_one_in, input_one),
+                (queries_in, queries),
+                (keys_in, keys),
+                (values_in, values),
+                (mixed_in, mixed),
+                (grad_mixed_in, grad_mixed),
+                (log_totals_in, log_totals),
+                (hidden_in, hidden),
+                (grad_middle_in, grad_middle),
+                (grad_attn_in, grad_attn),
+            )
+        )
+    ]
+    for load in loads:
+        load.start()
+
+    def weight_copy(at, slot):
+        return pltpu.make_async_copy(
+            whole_in.at[:, pl.ds(pl.multiple_of(at * tile, LANES), tile)],
+            weight_stage.at[slot],
+            weight_sem.at[slot],
+        )
+
+    def grad_copy(at, slot):
+        return pltpu.make_async_copy(
+            grad_stage.at[slot],
+            grad_low.at[:, pl.ds(pl.multiple_of(at * tile, LANES), tile)],
+            grad_sem.at[slot],
+        )
+
+    weight_copy(0, 0).start()
     greet_near()
-    away = pltpu.make_async_remote_copy(
-        src_ref=block_out,
-        dst_ref=block_swapped,
-        send_sem=swap_sem.at[0],
-        recv_sem=swap_sem.at[1],
-        device_id=near["swap"],
-        device_id_type=MESH,
-    )
-
-    @pl.when(jnp.logical_not(at_home))
-    def _():
-        away.start()
-
+    loads[0].wait()
     repeat(GRAD_SUBS, lambda at: reduce_step("across", refs, REDUCE_HIGH, sems, at))
 
     @pl.when(dp < 12)
     def _():
         owned[...] = jnp.zeros_like(owned)
+
+    for load in loads[1:]:
+        load.wait()
+
+    def flatten(source):
+        def go(at):
+            columns = pl.ds(pl.multiple_of(at * 256, LANES), 256)
+            flat_one[pl.ds(pl.multiple_of(at * 256, 256), 256)] = source[:, columns].T
+
+        repeat(D // 256, go)
+
+    flatten(input_one)
 
     def mates(pair):
         columns = pl.ds(pl.multiple_of(pair * LANES, LANES), LANES)
@@ -1453,7 +1573,6 @@
         ]
 
     def attention(pair):
-        reduce_step("tick", refs, REDUCE_HIGH, sems, pair)
         attend_back(
             pair,
             queries,
@@ -1468,6 +1587,7 @@
         )
         for mate in mates(pair):
             mate.start()
+        reduce_step("tick", refs, REDUCE_HIGH, sems, pair)
 
     repeat(PAIRS, attention)
     for source, target, total, index in (
@@ -1476,54 +1596,147 @@
     ):
         repeat(PAIRS, lambda pair: mates(pair)[index].wait())
         total[...] = (source[:HALF].astype(F32) + target[...].astype(F32)).astype(BF16)
-    repeat(
-        HIGH_STEPS - PAIRS, lambda at: reduce_step("tick", refs, REDUCE_HIGH, sems, at + PAIRS)
-    )
+
+    grad_one[...] = jnp.zeros_like(grad_one)
+
+    def project_back(source, base):
+        def go(at):
+            slot = lax.rem(at, 2)
+            weight_copy(at, slot).wait()
+
+            @pl.when(at + 1 < tiles)
+            def _():
+                weight_copy(at + 1, 1 - slot).start()
+
+            @pl.when(at >= 2)
+            def _():
+                grad_copy(at - 2, slot).wait()
+
+            columns = pl.ds(pl.multiple_of((at - base) * tile, LANES), tile)
+            for side in range(2):
+                part = slice(side * 512, (side + 1) * 512)
+                grad_one[:, part] += multiply(
+                    source[:, columns], weight_stage[slot, part], BOTH_LAST
+                )
+                narrow = pl.ds(pl.multiple_of((at - base) * tile + side * 256, LANES), 256)
+                grad_stage[slot, :, side * 256 : (side + 1) * 256] = multiply(
+                    flat_one[...], source[:, narrow]
+                ).astype(BF16)
+            grad_copy(at, slot).start()
+
+            @pl.when(at + PAIRS < HIGH_STEPS)
+            def _():
+                reduce_step("tick", refs, REDUCE_HIGH, sems, at + PAIRS)
+
+        def run(at, carried):
+            go(at + base)
+            return carried
+
+        lax.fori_loop(0, D // tile, run, 0)
+
+    project_back(grad_query, 0)
+    project_back(grad_key, D // tile)
+    project_back(grad_value, 2 * D // tile)
+
+    flatten(mixed)
+    for at in range(tiles, tiles + D // tile):
+        slot = at % 2
+        grad_copy(at - 2, slot).wait()
+        for side in range(2):
+            narrow = pl.ds((at - tiles) * tile + side * 256, 256)
+            grad_stage[slot, :, side * 256 : (side + 1) * 256] = multiply(
+                flat_one[...], grad_attn[:, narrow]
+            ).astype(BF16)
+        grad_copy(at, slot).start()
+    row_sums[...] = jnp.zeros_like(row_sums)
+
+    def shape_back(at):
+        rows = pl.ds(pl.multiple_of(at * 128, 128), 128)
+        value = hidden[rows].astype(F32)
+        center = value - jnp.mean(value, axis=-1, keepdims=True)
+        inverse = lax.rsqrt(jnp.mean(center * center, axis=-1, keepdims=True) + norm_eps)
+        normed = center * inverse
+        towards = grad_one[rows]
+        row_sums[0:1] += jnp.sum(towards, axis=0, keepdims=True)
+        row_sums[1:2] += jnp.sum(towards * normed, axis=0, keepdims=True)
+        row_sums[2:3] += jnp.sum(grad_query[rows].astype(F32), axis=0, keepdims=True)
+        row_sums[3:4] += jnp.sum(grad_value[rows].astype(F32), axis=0, keepdims=True)
+        scaled = towards * (1.0 + scale_one[...])
+        result = grad_middle[rows] + inverse * (
+            scaled
+            - jnp.mean(scaled, axis=-1, keepdims=True)
+            - normed * jnp.mean(scaled * normed, axis=-1, keepdims=True)
+        )
+        input_grad[rows] = result
+        input_low[rows] = result.astype(BF16)
+
+    repeat(4, shape_back)
+    for index in range(2):
+        sums[:, index * D : (index + 1) * D] = row_sums[index : index + 1]
+        start = 6 * D + WIDE + index * D
+        sums[:, start : start + D] = row_sums[index + 2 : index + 3]
+    sums[:, 2 * D : 6 * D] = early_sums[:, : 4 * D]
+    sums[:, 6 * D : 6 * D + WIDE] = jnp.zeros((1, WIDE), F32)
+    sums[:, 8 * D + WIDE :] = early_sums[:, 4 * D :]
+    for at in (tiles + D // tile - 2, tiles + D // tile - 1):
+        grad_copy(at, at % 2).wait()
     repeat(GRAD_SUBS, lambda at: reduce_step("drain", refs, REDUCE_HIGH, sems, at))
 
-    @pl.when(jnp.logical_not(at_home))
-    def _():
-        away.wait()
-
-
-def run_backward(queries, keys, values, mixed, grad_mixed, log_totals, grads, block_out):
+
+def run_backward(*given):
     shape = jax.ShapeDtypeStruct
     rows = TOKENS_HERE
     vmem = pl.BlockSpec(memory_space=pltpu.VMEM)
     hbm = pl.BlockSpec(memory_space=pl.ANY)
+    dma = pltpu.SemaphoreType.DMA
     return pl.pallas_call(
         backward_kernel,
-        out_shape=[shape((rows, D), BF16)] * 3
-        + [shape((HALF, WIDE), F32), shape((rows, D), BF16)],
-        in_specs=[vmem] * 7 + [hbm],
+        out_shape=[
+            shape((HALF, WIDE), F32),
+            shape((rows, D), F32),
+            shape((rows, D), BF16),
+            shape((1, VECTOR), F32),
+            shape((D, 4 * D), BF16),
+        ],
+        in_specs=[hbm] * 11 + [vmem] * 2 + [hbm],
         out_specs=[vmem] * 4 + [hbm],
-        scratch_shapes=[pltpu.VMEM((2 * rows, D), BF16)] * 2
+        scratch_shapes=[pltpu.VMEM(one.shape, one.dtype) for one in given[:11]]
+        + [dma((11,))]
+        + [pltpu.VMEM((rows, D), BF16)] * 3
+        + [pltpu.VMEM((8, D), F32)]
+        + [pltpu.VMEM((2 * rows, D), BF16)] * 2
         + [pltpu.VMEM((rows, D), BF16)] * 2
-        + [pltpu.SemaphoreType.DMA((PAIRS, 4)), pltpu.SemaphoreType.DMA((2,))]
-        + landing(BroadGrad, 1)
-        + landing_signals(BroadGrad, 1),
+        + [
+            pltpu.VMEM((D, rows), BF16),
+            pltpu.VMEM((2, D, 512), BF16),
+            pltpu.VMEM((2, D, 512), BF16),
+            pltpu.VMEM((rows, D), F32),
+            dma((PAIRS, 4)),
+            dma((2,)),
+            dma((2,)),
+        ]
+        + landing(HighGrad, 1)
+        + landing_signals(HighGrad, 1),
         compiler_params=pltpu.CompilerParams(
-            collective_id=1, has_side_effects=True, vmem_limit_bytes=60 * 2**20
+            collective_id=1, has_side_effects=True, vmem_limit_bytes=62 * 2**20
         ),
         cost_estimate=pl.CostEstimate(
-            flops=5 * 2 * 512 * 1024 * 1024 * 2, bytes_accessed=60 * 2**20, transcendentals=2**23
+            flops=12 * 2 * 512 * 1024 * 1024, bytes_accessed=60 * 2**20, transcendentals=2**23
         ),
         name="backward",
-    )(queries, keys, values, mixed, grad_mixed, log_totals, grads, block_out)
+    )(*given)
 
 
 VECTOR = 17 * WIDE
 
 
 def finish_kernel(
-    grad_qkv,
-    grad_out_proj,
+    grad_low,
     grad_up,
     low_in,
     active_rows,
     condition,
     sums,
-    input_grad,
     owned_high,
     down_sum,
     owned,
@@ -1531,7 +1744,6 @@
     bias_parts,
     ada_bias_grad,
     owned_down,
-    input_swapped,
     grads,
     ada_weights,
     sum_mate,
@@ -1548,7 +1760,6 @@
     bias_recv,
     cond_send,
     cond_recv,
-    swap_sem,
     *scratch,
 ):
     z, x, c, y = place()
@@ -1559,7 +1770,6 @@
         "NarrowGrad": (grads, 0, owned, scratch[7:14]),
     }
     sems = {"BroadGrad": scratch[14:16], "NarrowGrad": scratch[16:18]}
-    at_home = c == y
 
     def remote(source, target, sent, arrived, device):
         return pltpu.make_async_remote_copy(
@@ -1572,12 +1782,11 @@
         )
 
     loads = [
-        pltpu.make_async_copy(grad_qkv, grads.at[:, : 3 * D], local_sem.at[0]),
-        pltpu.make_async_copy(grad_out_proj, grads.at[:, 3 * D : 4 * D], local_sem.at[1]),
+        pltpu.make_async_copy(grad_low, grads.at[:, : 4 * D], local_sem.at[0]),
         pltpu.make_async_copy(
-            grad_up.at[:, :HIGH_FIRST], grads.at[:, 4 * D : 4 * D + HIGH_FIRST], local_sem.at[2]
+            grad_up.at[:, :HIGH_FIRST], grads.at[:, 4 * D : 4 * D + HIGH_FIRST], local_sem.at[1]
         ),
-        pltpu.make_async_copy(low_in.at[pl.ds(0, HALF)], ada_weights, local_sem.at[3]),
+        pltpu.make_async_copy(low_in.at[pl.ds(0, HALF)], ada_weights, local_sem.at[2]),
     ]
     for load in loads:
         load.start()
@@ -1593,11 +1802,11 @@
         near["y"],
     )
     down_away.start()
-    away = remote(input_grad, input_swapped, swap_sem.at[0], swap_sem.at[1], near["swap"])
-
-    for load in loads[:3]:
+
+    for load in loads[:2]:
         load.wait()
     repeat(GRAD_SUBS, lambda at: reduce_step("across", refs, REDUCE_LOW, sems, at))
+    repeat(2, lambda at: reduce_step("tick", refs, REDUCE_LOW, sems, at))
 
     mate.wait()
     for index in range(17):
@@ -1641,11 +1850,7 @@
         repeat(17, go)
 
     each_piece(lambda copy: copy.start(), True)
-    repeat(3, lambda at: reduce_step("tick", refs, REDUCE_LOW, sems, at))
-
-    @pl.when(jnp.logical_not(at_home))
-    def _():
-        away.start()
+    repeat(3, lambda at: reduce_step("tick", refs, REDUCE_LOW, sems, at + 2))
 
     def from_latent(at, target, arrived):
         mine = (at // 2 == z * 2 + x) & (lax.rem(at, 2) == y) & (c == y)
@@ -1656,7 +1861,7 @@
                 sum_pieces.at[0], target.at[at], piece_send.at[0], arrived.at[at], near["x"]
             ).wait_recv()
 
-    loads[3].wait()
+    loads[2].wait()
 
     @pl.when(dp < 7)
     def _():
@@ -1702,7 +1907,7 @@
     def _():
         each_cond(lambda copy: copy.start(), True)
 
-    repeat(LOW_STEPS - 3, lambda at: reduce_step("tick", refs, REDUCE_LOW, sems, at + 3))
+    repeat(LOW_STEPS - 5, lambda at: reduce_step("tick", refs, REDUCE_LOW, sems, at + 5))
 
     def cond_arrived(at):
         @pl.when(at != dp * 2 + y)
@@ -1732,10 +1937,6 @@
     def _():
         bias_parts[...] = jnp.zeros_like(bias_parts)
 
-    @pl.when(jnp.logical_not(at_home))
-    def _():
-        away.wait()
-
     down_away.wait()
     owned_down[...] = down_sum[
         :, pl.ds(pl.multiple_of(y * FF_PART, LANES), FF_PART)
@@ -1750,14 +1951,12 @@
 
 
 def run_finish(
-    grad_qkv,
-    grad_out_proj,
+    grad_low,
     grad_up,
     low_in,
     active_rows,
     condition,
     sums,
-    input_grad,
     owned_high,
     down_sum,
 ):
@@ -1773,10 +1972,9 @@
             shape((DP, 1, WIDE), F32),
             shape((1, WIDE), F32),
             shape((64, FF_PART), F32),
-            shape((TOKENS_HERE, D), BF16),
         ],
-        in_specs=[hbm] * 4 + [vmem] * 3 + [hbm, vmem, vmem],
-        out_specs=[vmem] * 5 + [hbm],
+        in_specs=[hbm] * 3 + [vmem] * 5,
+        out_specs=[vmem] * 5,
         scratch_shapes=[
             pltpu.VMEM((D, 4 * D + HIGH_FIRST), BF16),
             pltpu.VMEM((HALF, WIDE), BF16),
@@ -1786,7 +1984,7 @@
             pltpu.VMEM((DP, 1, HALF), F32),
             pltpu.VMEM((14, 1, HALF), F32),
             pltpu.VMEM((64, FF_PART), BF16),
-            dma((4,)),
+            dma((3,)),
             dma((2,)),
             dma((2,)),
             dma((17,)),
@@ -1794,7 +1992,6 @@
             dma((DP,)),
             dma((2 * DP,)),
             dma((14,)),
-            dma((2,)),
         ]
         + landing(BroadGrad, 2)
         + landing(NarrowGrad, 1)
@@ -1805,17 +2002,24 @@
         ),
         name="finish",
     )(
-        grad_qkv,
-        grad_out_proj,
+        grad_low,
         grad_up,
         low_in,
         active_rows,
         condition,
         sums,
-        input_grad,
         owned_high,
         down_sum,
     )
+
+
+def swap_away(values):
+    pairs = []
+    for index in range(2 * DP):
+        y, c = index % 2, index // 2 % 2
+        if y != c:
+            pairs.append((index, index // 4 * 4 + y * 2 + c))
+    return lax.ppermute(values, ("dp", "seq"), pairs)
 
 
 def local(
@@ -1857,7 +2061,7 @@
         input_two,
         slope,
         grad_branch,
-        gate_two_grad,
+        row_grads,
         block_out,
         grad_down,
     ) = run_forward(
@@ -1868,6 +2072,8 @@
         cond_float,
         bias_row[:1].astype(F32),
     )
+    at_home = lax.rem(dp, 2) == y
+    block_swapped = swap_away(block_out)
     grad_out = grad_out.astype(F32)
     pieces = [modulation[:, part * D : (part + 1) * D] for part in range(6)]
     shift_one, scale_one, gate_one, shift_two, scale_two, gate_two = pieces
@@ -1897,54 +2103,53 @@
     grad_middle = grad_out + norm_pull_two(grad_input_two * (1.0 + scale_two))[0]
     grad_attn = (grad_middle * gate_one).astype(BF16)
     gate_one_grad = down_rows(grad_middle * attn_out)
-    grad_out_proj = outer(mixed, grad_attn).astype(BF16)
     grad_mixed = back_through(grad_attn, 3 * D, D).astype(BF16)
-    at_home = lax.rem(dp, 2) == y
-    grad_query, grad_key, grad_value, owned_high, block_swapped = run_backward(
-        queries, keys, values, mixed, grad_mixed, log_totals, grad_up, block_out
-    )
-    block_out = jnp.where(at_home, block_out, block_swapped)
-    grad_qkv = jnp.concatenate([grad_query, grad_key, grad_value], axis=-1)
-    grad_proj_qkv = outer(input_one, grad_qkv).astype(BF16)
-    grad_input_one = back_through(grad_qkv, 0, 3 * D)
-    normed_one, norm_pull_one = jax.vjp(layer_norm, hidden.astype(F32))
-    shift_one_grad = down_rows(grad_input_one)
-    scale_one_grad = down_rows(grad_input_one * normed_one)
-    input_grad = grad_middle + norm_pull_one(grad_input_one * (1.0 + scale_one))[0]
-    sums = jnp.concatenate(
+    early_sums = jnp.concatenate(
         [
-            shift_one_grad,
-            scale_one_grad,
             gate_one_grad,
             shift_two_grad,
             scale_two_grad,
-            gate_two_grad,
-            jnp.zeros((1, WIDE), F32),
-            down_rows(grad_query),
-            down_rows(grad_value),
+            row_grads[0:1],
             down_rows(grad_attn),
             down_rows(grad_upward),
-            down_rows(grad_branch),
+            row_grads[1:2],
         ],
         axis=-1,
     )
+    owned_high, input_grad, input_low, sums, grad_low = run_backward(
+        queries,
+        keys,
+        values,
+        mixed,
+        grad_mixed,
+        log_totals,
+        grad_up,
+        input_one,
+        hidden,
+        grad_middle,
+        grad_attn,
+        scale_one,
+        early_sums,
+        whole_in,
+    )
     active_rows = lax.dynamic_slice_in_dim(
         jax.nn.silu(cond_all[:, 0]).astype(BF16), y * HALF, HALF, 1
     )
-    owned_in, cond_grad, bias_parts, ada_bias_grad, owned_down, input_swapped = run_finish(
-        grad_proj_qkv,
-        grad_out_proj,
+    owned_in, cond_grad, bias_parts, ada_bias_grad, owned_down = run_finish(
+        grad_low,
         grad_up,
         low_in,
         active_rows,
         cond_float,
         sums,
-        input_grad.astype(BF16),
         owned_high,
         down_sum,
     )
     owned_down = owned_down.T
+    input_low, owned_in = lax.optimization_barrier((input_low, owned_in))
+    input_swapped = swap_away(input_low)
     input_grad = jnp.where(at_home, input_grad, input_swapped.astype(F32))
+    block_out = jnp.where(at_home, block_out, block_swapped)
     owned_bias = jnp.sum(bias_parts[:, 0], axis=0) + ada_bias_grad[0]
     owned_bias = lax.dynamic_slice_in_dim(owned_bias, y * side, side, 0)
     moments_in, squares_in, master_in = adamw_step(

time: 449 us -> 422 us (0.940)
  Pallas kernels: 347 us -> 330 us
  matrix products: 43.1 us -> 27.9 us
    pallas_call x1, Pallas kernels: 164 us -> 154 us  [run_forward(): pl.pallas_call(forward_kernel, out_shape=[one for one, _ in outs], in_spe...]
    pallas_call x1, Pallas kernels: 83.7 us -> 74.5 us  [run_finish(): pl.pallas_call(finish_kernel, out_shape=[shape((HALF, WIDE), F32), shape(...]
    dot_general x3 -> x1, matrix products: 15.1 us -> 6.81 us  [outer(): return lax.dot_general(left, right, BOTH_FIRST, preferred_element_type=F32)]
    dot_general x3 -> x2, matrix products: 18.6 us -> 11.7 us  [back_through(): lax.dot_general(gradients, whole_in[:, start:start + width], BOTH_LAST, p...]
  transfers between devices with their start and end apart: 1 -> 3, of which waited for: 0 -> 1; matrix products, arithmetic and copies ran while one was open for 12% -> 11% of each run, Pallas kernels for 23% -> 25%
where the time goes in v3:
time: 422 us; the launch traced here: 413 us
  Pallas kernels  330 us (78%)
  matrix products  27.9 us (7%)
  other arithmetic  26.4 us (6%)
  between operations  14.8 us (4%)
  local copies, waits for them, and re-layouts  6.07 us (1%)
    pallas_call x1, Pallas kernels, run_forward(): pl.pallas_call(forward_kernel, out_shape=[one for one, _ in outs], in_spe...  154 us
    pallas_call x1, Pallas kernels, run_backward(): pl.pallas_call(backward_kernel, out_shape=[shape((HALF, WIDE), F32), shap...  102 us
    pallas_call x1, Pallas kernels, run_finish(): pl.pallas_call(finish_kernel, out_shape=[shape((HALF, WIDE), F32), shape(...  74.5 us
    dot_general x2, matrix products, back_through(): lax.dot_general(gradients, whole_in[:, start:start + width], BOTH_LAST, p...  11.7 us
    dot_general x1, matrix products, local(): grad_act = jnp.dot(grad_branch, whole_down, preferred_element_type=F32)  9.46 us
  transfers between devices with their start and end apart: 3, of which 1 were waited for; matrix products, arithmetic and copies ran while one was open for 11% of the time, Pallas kernels for 25%

profile of v3, /device:TPU:19, one launch (start us, length us, event | category | flops | bytes accessed | tf_op | source)
XLA Modules:
  0.0 413.2 jit_solution(2115405633078653322)
XLA Ops:
  7.9 1.3 convert_element_type.56.condition
  9.9 1.8 convert_bitcast_fusion.low_down
  11.7 1.6 convert_element_type.53
  13.3 1.0 pad_maximum_fusion.low_in
  14.3 153.5 %forward.1 = (bf16[1024,8192]{1,0:T(8,128)(2,1)}, bf16[1024,4096]{1,0:T(8,128)(2,1)}, bf16[512,1024]{1,0:T(8,128)(2,1)}, bf16[512,1024]{1,0:T(8,128)(2,1)}, f32[...) custom-call(bf16[528,896]{1,0:T(8,128)(2,1)} %pad_maximum_fusion.low, ...), custom_call_target="tpu_custom_call" | custom-call | tf_op jit(solution)/shard_map/forward/pallas_call | solution.py:1137
  167.8 1.2 copy-done.7
  169.0 2.1 collective-permute-start
  171.7 1.3 fusion.18
  173.0 9.5 %convert_reduce_fusion = (f32[4096]{0:T(1024)S(1)}, bf16[512,4096]{1,0:T(8,128)(2,1)S(1)}) fusion(f32[512,4096]{1,0:T(8,128)} %get-tuple-element.55, bf16[512,1024]{1,0:T(8,128)(2,1)S(1)} %copy-done.17, bf16[1024,4096]{1,0:T(8,128)(2,1)} %get-tuple-element.54), kind=kOutput, calls=%fused_computation | convolution fusion | flops 4303351808 | bytes 22036480 | tf_op jit(solution)/shard_map/dot_general | solution.py:2096
  182.5 7.5 %multiply_reduce_fusion = (f32[1024]{0:T(1024)S(1)}, f32[512]{0:T(512)S(1)}, f32[1024]{0:T(1024)S(1)}, f32[512,1024]{1,0:T(8,128)S(1)}) fusion(f32[512,1024]{1,0:T(8,128)S(1)} %copy-done, f32[512]{0:T(512)S(1)} %fusion.10, f32[512]{0:T(512)S(1)} %broadcast_multiply_fusion, f32[1024]{0:T(1024)S(1)} %bitcast.36, ...), kind=kOutput, calls=%fused_computation.10 | convolution fusion | flops 4299159040 | bytes 16795648 | tf_op jit(solution)/shard_map/dot_general | solution.py:2082
  191.8 2.0 copy-done.3
  194.4 0.8 constant_dynamic-update-slice_fusion.3
  195.8 0.8 constant_dynamic-update-slice_fusion.early_sums
  196.6 4.2 %fusion.5.grad_mixed_in = bf16[512,1024]{1,0:T(8,128)(2,1)} fusion(bf16[512,1024]{1,0:T(8,128)(2,1)S(1)} %get-tuple-element.95.grad_attn_in, bf16[1024,8192]{1,0:T(8,128)(2,1)} %get-tuple-element.56.whole_in), kind=kOutput, calls=%fused_computation.20 | convolution fusion | flops 1074266112 | bytes 4194304 | tf_op jit(solution)/shard_map/dot_general | solution.py:2082
  200.8 6.8 %convolution_convert_fusion.grads_in.grad_up = bf16[1024,4096]{1,0:T(8,128)(2,1)} fusion(bf16[512,1024]{1,0:T(8,128)(2,1)S(1)} %copy-done.16, bf16[512,4096]{1,0:T(8,128)(2,1)S(1)} %get-tuple-element.104), kind=kOutput, calls=%fused_computation.4 | convolution fusion | flops 4299161600 | bytes 13631488 | tf_op jit(solution)/shard_map/dot_general | solution.py:2090
  207.6 101.9 %backward.1 = (f32[512,896]{1,0:T(8,128)}, f32[512,1024]{1,0:T(8,128)}, bf16[512,1024]{1,0:T(8,128)(2,1)}, f32[1,15232]{1,0:T(1,128)}, bf16[1024,4096]{1,0:T(8,128)(2,1)}) custom-call(bf16[512,1024]{1,0:T(8,128)(2,1)} %get-tuple-element.48.queries_in, bf16[1024,1024]{1,0:T(8,128)(2,1)} %get-tuple-element.49.keys_in, ...), custom_call_target="tpu_custom_call" | custom-call | flops 12884901888 | bytes 62914560 | tf_op jit(solution)/shard_map/backward/pallas_call | solution.py:1692
  309.6 2.3 select_bitcast_fusion.1
  311.9 74.5 %finish.1 = (f32[512,896]{1,0:T(8,128)}, f32[1,1024]{1,0:T(1,128)}, f32[16,1,896]{2,1,0:T(1,128)}, f32[1,896]{1,0:T(1,128)}, f32[64,2048]{1,0:T(8,128)}) custom-call(bf16[1024,4096]{1,0:T(8,128)(2,1)} %get-tuple-element.67.grad_low, bf16[1024,4096]{1,0:T(8,128)(2,1)} %convolution_convert_fusion.grads_in.grad_up, bf16[528,896]{1,0:T(8,128)(2,1)} %pad_maximum_fusion.low_in, ...), custom_call_target="tpu_custom_call" | custom-call | tf_op jit(solution)/shard_map/finish/pallas_call | solution.py:1967
  386.4 1.0 reduce_sum.107
  387.4 1.9 collective-permute-start.1
  390.8 2.9 fusion.13
  393.6 5.9 %fusion.15 = (bf16[512,896]{1,0:T(8,128)(2,1)}, f32[512,896]{1,0:T(8,128)}, f32[512,896]{1,0:T(8,128)}, f32[512,896]{1,0:T(8,128)}) fusion(f32[512,896]{1,0:T(8,128)S(1)} %copy-done.2, f32[512,896]{1,0:T(8,128)} %get-tuple-element.75, f32[512,896]{1,0:T(8,128)S(1)} %copy-done.6, f32[512,896]{1,0:T(8,128)} %param.18), kind=kLoop, calls=%fused_computation.52 | loop fusion | flops 6881280 | bytes 13762560 | tf_op jit(solution)/shard_map/convert_element_type | solution.py:2177
  399.6 4.1 %collective-permute-done.1 = bf16[512,1024]{1,0:T(8,128)(2,1)S(1)} collective-permute-done((bf16[512,1024]{1,0:T(8,128)(2,1)}, bf16[512,1024]{1,0:T(8,128)(2,1)S(1)}, u32[]{:S(2)}, u32[]{:S(2)}) %collective-permute-start.1) | collective-permute-done | bytes 1048608 | tf_op jit(solution)/shard_map/ppermute | solution.py:2022
  403.7 1.6 select_bitcast_fusion
  (63 shorter events, 7.1 us)
Async XLA Ops:
  7.2 304.7 %reduce-scatter.2.cloned.1.call-start = ((), (), s32[]{:S(2)}) async-start(), calls=%async_computation.1 | async-start | bytes 8912896 | tf_op jit(solution)/shard_map/reduce_scatter | solution.py:2095
  167.8 1.2 copy-start.7
  167.8 3.3 copy-start.10
  167.8 3.3 copy-start
  169.0 140.6 %collective-permute-start = (bf16[512,1024]{1,0:T(8,128)(2,1)S(1)}, bf16[512,1024]{1,0:T(8,128)(2,1)}, u32[]{:S(2)}, u32[]{:S(2)}) collective-permute-start(bf16[512,1024]{1,0:T(8,128)(2,1)S(1)} %copy-done.7), channel_id=1, source_target_pairs={{1,2},{2,1},{5,6},{6,5},{9,10},{10,9},{13,14},{14,13},{17,18},{18,... | collective-permute-start | bytes 3145736 | tf_op jit(solution)/shard_map/ppermute | solution.py:2022
  171.3 1.7 copy-start.17
  190.0 1.4 copy-start.8
  191.3 2.5 copy-start.3
  191.8 2.6 copy-start.1
  191.8 4.8 %copy-start.9 = (bf16[512,1024]{1,0:T(8,128)(2,1)}, bf16[512,1024]{1,0:T(8,128)(2,1)S(1)}, u32[]{:S(2)}) copy-start(bf16[512,1024]{1,0:T(8,128)(2,1)S(1)} %get-tuple-element.95.grad_attn_in) | copy-start | bytes 3145732
  196.6 4.2 %copy-start.15 = (f32[1,10240]{1,0:T(1,128)}, f32[1,10240]{1,0:T(1,128)S(1)}, u32[]{:S(2)}) copy-start(f32[1,10240]{1,0:T(1,128)S(1)} %constant_dynamic-update-slice_fusion.early_sums) | copy-start | bytes 122884
  196.6 4.2 %copy-start.16 = (bf16[512,1024]{1,0:T(8,128)(2,1)S(1)}, bf16[512,1024]{1,0:T(8,128)(2,1)}, u32[]{:S(2)}) copy-start(bf16[512,1024]{1,0:T(8,128)(2,1)} %get-tuple-element.60) | copy-start | bytes 3145732
  311.9 78.2 %copy-start.11 = (f32[448]{0:T(512)S(1)}, f32[448]{0:T(512)}, u32[]{:S(2)}) copy-start(f32[448]{0:T(512)} %param.17) | copy-start | bytes 5380
  311.9 78.2 %copy-start.13 = (f32[448]{0:T(512)S(1)}, f32[448]{0:T(512)}, u32[]{:S(2)}) copy-start(f32[448]{0:T(512)} %param.23) | copy-start | bytes 5380
  311.9 78.2 %copy-start.14 = (f32[448]{0:T(512)S(1)}, f32[448]{0:T(512)}, u32[]{:S(2)}) copy-start(f32[448]{0:T(512)} %param.20) | copy-start | bytes 5380
  311.9 78.9 %copy-start.4 = (f32[2048,64]{0,1:T(8,128)S(1)}, f32[2048,64]{0,1:T(8,128)}, u32[]{:S(2)}) copy-start(f32[2048,64]{0,1:T(8,128)} %param.16) | copy-start | bytes 1572868
  386.4 7.2 %copy-start.2 = (f32[512,896]{1,0:T(8,128)S(1)}, f32[512,896]{1,0:T(8,128)}, u32[]{:S(2)}) copy-start(f32[512,896]{1,0:T(8,128)} %param.15) | copy-start | bytes 5505028
  387.4 16.3 %collective-permute-start.1 = (bf16[512,1024]{1,0:T(8,128)(2,1)}, bf16[512,1024]{1,0:T(8,128)(2,1)S(1)}, u32[]{:S(2)}, u32[]{:S(2)}) collective-permute-start(bf16[512,1024]{1,0:T(8,128)(2,1)} %get-tuple-element.73), channel_id=1, source_target_pairs={{1,2},{2,1},{5,6},{6,5},{9,10},{10,9},{13,14},{14,13},{17,18},{18,... | collective-permute-start | bytes 3145736 | tf_op jit(solution)/shard_map/ppermute | solution.py:2022
  390.0 3.6 copy-start.6
  393.6 10.1 %copy-start.5 = (f32[512,1024]{1,0:T(8,128)S(1)}, f32[512,1024]{1,0:T(8,128)}, u32[]{:S(2)}) copy-start(f32[512,1024]{1,0:T(8,128)} %get-tuple-element.65) | copy-start | bytes 6291460
  403.7 1.6 copy-start.12
Sparse Core Ops, SparseCore 0:
  167.9 130.7 reduce-scatter.1
